TPU v7x, 512 devices: a whole 4x8x8 slice. The times are simulated.
512 devices in a mesh: dp: 4 (over y_hi, core), seq: 128 (over x, z, y_lo).
Axes of the slice: x: 4, y: 8 (y_hi: 2, y_lo: 4; y = y_hi * 4 + y_lo), z: 8, core: 2. Of those that a mesh axis runs over, the one named last changes fastest.
Arguments:
- queries: bfloat16 [65536, 768], P(('dp', 'seq')), parts along dimension 0, may hold values from -6 to 6
- keys: bfloat16 [65536, 768], P(('dp', 'seq')), parts along dimension 0, may hold values from -6 to 6
- values: bfloat16 [65536, 768], P(('dp', 'seq')), parts along dimension 0, may hold values from -16 to 16
- cotangent: bfloat16 [65536, 768], P(('dp', 'seq')), parts along dimension 0, may hold values from -24 to 24
- out_weight: bfloat16 [768, 768], replicated, may hold values from -0.21875 to 0.21875
- slide_lengths: int32 [32], P('dp'), parts along dimension 0, may hold values from 1 to 4096, 16384 in all
- head_dilation_shifts: int32 [2, 16], replicated, may hold values from 0 to 15, as said below
Outputs:
- mixed: bfloat16 [65536, 768], P(('dp', 'seq')), parts along dimension 0
- grad_queries: bfloat16 [65536, 768], P(('dp', 'seq')), parts along dimension 0
- grad_keys: bfloat16 [65536, 768], P(('dp', 'seq')), parts along dimension 0
- grad_values: bfloat16 [65536, 768], P(('dp', 'seq')), parts along dimension 0
- out_weight_grad: float32 [3072, 768], P(('dp', 'seq')), parts along dimension 0
There are 4 independent parts, one for each index of `dp`. A program takes and returns all parts, laid end to end along the dimension named above; an argument that names none is the same for every part. Nothing has to cross between parts.
Inputs may be any that keep to these rules, and one draw needn't show every extreme that they name: `head_dilation_shifts`: row 0 holds each head's offset at level two, below 4; row 1 each head's offset at level three, below 16.
All inputs are finite; a program needn't handle non-finite values.
Results may differ from a plain program's by a relative error of at most 0.012.
The roundings to bfloat16 on the way count: a program that leaves them out, or rounds other values in their place, can miss the bound.
Values may be sent and summed in bfloat16 or wider, within the bound.
A program may use at most 64 MiB of HBM per device.

v0:
```python
import jax
import jax.numpy as jnp
import numpy as np
from jax import lax
from jax.sharding import PartitionSpec as P

ATTENTION_HEADS = 16
DILATION_TWO = 4
DILATION_THREE = 16
REACH_TWO = 8
REACH_THREE = 32


def from_partner(value, axis, distance):
    mask = 2**distance
    pairs = [(source, source ^ mask) for source in range(lax.axis_size(axis))]
    return lax.ppermute(value, axis, pairs)


def slide_index(positions, slide_ends):
    return jnp.sum((positions[..., None] >= slide_ends).astype(jnp.int32), axis=-1)


def pick(array, rate, shifts):
    if rate == 1:
        return array
    rows = array.reshape((array.shape[0] // rate, rate) + array.shape[1:])
    chosen = jnp.arange(rate, dtype=jnp.int32)[:, None] == shifts[None, :]
    chosen = chosen.reshape(chosen.shape + (1,) * (array.ndim - 2))
    return jnp.sum(jnp.where(chosen[None], rows, jnp.zeros((), array.dtype)), axis=1)


def spread(selected, rate, shifts, fill):
    if rate == 1:
        return selected
    chosen = jnp.arange(rate, dtype=jnp.int32)[:, None] == shifts[None, :]
    chosen = chosen.reshape(chosen.shape + (1,) * (selected.ndim - 2))
    wide = jnp.where(chosen[None], selected[:, None], fill)
    return wide.reshape((selected.shape[0] * rate,) + selected.shape[1:])


def owner_table(bit_list):
    return np.array(
        [
            sum(((block >> place & 1) << bit for place, bit in enumerate(bit_list)))
            for block in range(1 << len(bit_list))
        ],
        np.int32,
    )


def join_pair(mine, other, upper):
    return jnp.where(
        upper, jnp.concatenate([other, mine], axis=1), jnp.concatenate([mine, other], axis=1)
    )


def double_up(pieces, bit_lists, order, rank):
    pieces = list(pieces)
    for bit in order:
        active = [index for index in range(len(pieces)) if bit in bit_lists[index]]
        upper = rank >> bit & 1 == 1
        for index in active:
            other = from_partner(pieces[index], "seq", bit)
            pieces[index] = join_pair(pieces[index], other, upper)
    return pieces


def fold_down(pieces, bit_lists, order, rank):
    pieces = list(pieces)
    for bit in reversed(order):
        active = [index for index in range(len(pieces)) if bit in bit_lists[index]]
        upper = rank >> bit & 1 == 1
        kept, sent = ([], [])
        for index in active:
            piece = pieces[index]
            halves = piece.reshape(2, 2, piece.shape[1] // 2, piece.shape[2])
            kept.append(jnp.where(upper, halves[:, 1], halves[:, 0]))
            sent.append(jnp.where(upper, halves[:, 0], halves[:, 1]))
        for index, keep, send in zip(active, kept, sent):
            pieces[index] = keep + from_partner(send.astype(jnp.bfloat16), "seq", bit).astype(
                send.dtype
            )
    return pieces


def attend(query_rows, key_rows, value_rows, query_slides, key_slides, scale):
    scores = (
        jnp.einsum("qhd,khd->hqk", query_rows, key_rows, preferred_element_type=jnp.float32) * scale
    )
    visible = query_slides.T[:, :, None] == key_slides.T[:, None, :]
    highest = jnp.max(jnp.where(visible, scores, -jnp.inf), axis=-1)
    weights = jnp.where(visible, jnp.exp(scores - highest[..., None]), 0.0)
    totals = jnp.sum(weights, axis=-1)
    summed = jnp.einsum(
        "hqk,khd->qhd", weights.astype(jnp.bfloat16), value_rows, preferred_element_type=jnp.float32
    )
    return (highest.T, totals.T, summed)


def score_grads(
    query_rows,
    key_rows,
    value_rows,
    grad_rows,
    lse_rows,
    delta_rows,
    query_slides,
    key_slides,
    scale,
):
    scores = (
        jnp.einsum("qhd,khd->hqk", query_rows, key_rows, preferred_element_type=jnp.float32) * scale
    )
    visible = query_slides.T[:, :, None] == key_slides.T[:, None, :]
    probs = jnp.where(visible, jnp.exp(scores - lse_rows.T[:, :, None]), 0.0)
    dprobs = jnp.einsum("qhd,khd->hqk", grad_rows, value_rows, preferred_element_type=jnp.float32)
    dscores = (probs * (dprobs - delta_rows.T[:, :, None]) * scale).astype(jnp.bfloat16)
    return (probs, dscores)


def attend_back(
    query_rows,
    key_rows,
    value_rows,
    grad_rows,
    lse_rows,
    delta_rows,
    query_slides,
    key_slides,
    scale,
):
    probs, dscores = score_grads(
        query_rows,
        key_rows,
        value_rows,
        grad_rows,
        lse_rows,
        delta_rows,
        query_slides,
        key_slides,
        scale,
    )
    grad_q = jnp.einsum("hqk,khd->qhd", dscores, key_rows, preferred_element_type=jnp.float32)
    grad_k = jnp.einsum("hqk,qhd->khd", dscores, query_rows, preferred_element_type=jnp.float32)
    grad_v = jnp.einsum(
        "hqk,qhd->khd", probs.astype(jnp.bfloat16), grad_rows, preferred_element_type=jnp.float32
    )
    return (grad_q, grad_k, grad_v)


def local(queries, keys, values, cotangent, out_weight, slide_lengths, head_dilation_shifts):
    tok_dev, width = queries.shape
    head_dim = width // ATTENTION_HEADS
    scale = head_dim ** (-0.5)
    sequence_count = lax.axis_size("seq")
    rank = lax.axis_index("seq")
    slide_ends = jnp.cumsum(slide_lengths)
    level_layouts = [
        (1, 1, jnp.zeros((ATTENTION_HEADS,), jnp.int32)),
        (DILATION_TWO, min(REACH_TWO, sequence_count), head_dilation_shifts[0]),
        (DILATION_THREE, min(REACH_THREE, sequence_count), head_dilation_shifts[1]),
    ]
    widest = max((group.bit_length() - 1 for rate, group, shifts in level_layouts))
    order = list(range(widest))
    bit_lists = [
        [bit for bit in order if bit < group.bit_length() - 1]
        for rate, group, shifts in level_layouts
    ]
    views = [array.reshape(tok_dev, ATTENTION_HEADS, head_dim) for array in (queries, keys, values)]
    picked_all = []
    outgoing = []
    for rate, group, shifts in level_layouts:
        picked = [pick(array, rate, shifts) for array in views]
        picked_all.append(picked)
        outgoing.append(jnp.stack([picked[1], picked[2]]).reshape(2, tok_dev // rate, width))
    arrived = double_up(outgoing, bit_lists, order, rank)
    layouts = []
    highs, sums, partials = ([], [], [])
    for index, (rate, group, shifts) in enumerate(level_layouts):
        count = tok_dev // rate
        row_offsets = jnp.arange(count, dtype=jnp.int32)[:, None] * rate + shifts[None, :]
        query_slides = slide_index(rank * tok_dev + row_offsets, slide_ends)
        owners = jnp.asarray(owner_table(bit_lists[index]), jnp.int32)
        base = rank - rank % group
        key_positions = ((base + owners)[:, None, None] * tok_dev + row_offsets[None]).reshape(
            -1, ATTENTION_HEADS
        )
        key_slides = slide_index(key_positions, slide_ends)
        gathered = arrived[index].reshape(2, -1, ATTENTION_HEADS, head_dim)
        layouts.append((gathered, query_slides, key_slides))
        highest, totals, summed = attend(
            picked_all[index][0], gathered[0], gathered[1], query_slides, key_slides, scale
        )
        highs.append(spread(highest, rate, shifts, -jnp.inf))
        sums.append(spread(totals, rate, shifts, 0.0))
        partials.append(spread(summed, rate, shifts, 0.0))
    best = highs[0]
    for highest in highs[1:]:
        best = jnp.maximum(best, highest)
    mass = jnp.zeros((tok_dev, ATTENTION_HEADS), jnp.float32)
    for highest, totals in zip(highs, sums):
        mass = mass + jnp.exp(highest - best) * totals
    lse = best + jnp.log(mass)
    combined = jnp.zeros((tok_dev, ATTENTION_HEADS, head_dim), jnp.float32)
    for highest, summed in zip(highs, partials):
        combined = combined + jnp.exp(highest - lse)[..., None] * summed
    attended = combined.reshape(tok_dev, width).astype(jnp.bfloat16)
    mixed = lax.dot_general(
        attended, out_weight, (((1,), (1,)), ((), ())), preferred_element_type=jnp.float32
    ).astype(jnp.bfloat16)
    d_attended = jnp.dot(cotangent, out_weight, preferred_element_type=jnp.float32).astype(
        jnp.bfloat16
    )
    delta = jnp.sum(
        (d_attended.astype(jnp.float32) * attended.astype(jnp.float32)).reshape(
            tok_dev, ATTENTION_HEADS, head_dim
        ),
        axis=-1,
    )
    d_view = d_attended.reshape(tok_dev, ATTENTION_HEADS, head_dim)
    grad_query_total = jnp.zeros((tok_dev, ATTENTION_HEADS, head_dim), jnp.float32)
    grad_key_total = jnp.zeros((tok_dev, ATTENTION_HEADS, head_dim), jnp.float32)
    grad_value_total = jnp.zeros((tok_dev, ATTENTION_HEADS, head_dim), jnp.float32)
    returning = []
    for index, (rate, group, shifts) in enumerate(level_layouts):
        gathered, query_slides, key_slides = layouts[index]
        grad_q, grad_k, grad_v = attend_back(
            picked_all[index][0],
            gathered[0],
            gathered[1],
            pick(d_view, rate, shifts),
            pick(lse, rate, shifts),
            pick(delta, rate, shifts),
            query_slides,
            key_slides,
            scale,
        )
        grad_query_total = grad_query_total + spread(grad_q, rate, shifts, 0.0)
        returning.append(jnp.stack([grad_k, grad_v]).reshape(2, -1, width))
    folded = fold_down(returning, bit_lists, order, rank)
    for index, (rate, group, shifts) in enumerate(level_layouts):
        mine = folded[index].reshape(2, tok_dev // rate, ATTENTION_HEADS, head_dim)
        grad_key_total = grad_key_total + spread(mine[0], rate, shifts, 0.0)
        grad_value_total = grad_value_total + spread(mine[1], rate, shifts, 0.0)
    out_weight_grad = lax.psum_scatter(
        lax.dot_general(
            cotangent, attended, (((0,), (0,)), ((), ())), preferred_element_type=jnp.float32
        ),
        "seq",
        scatter_dimension=0,
        tiled=True,
    ) * (tok_dev * sequence_count) ** (-0.5)
    grad_queries = grad_query_total.reshape(tok_dev, width).astype(jnp.bfloat16)
    grad_keys = grad_key_total.reshape(tok_dev, width).astype(jnp.bfloat16)
    grad_values = grad_value_total.reshape(tok_dev, width).astype(jnp.bfloat16)
    return (mixed, grad_queries, grad_keys, grad_values, out_weight_grad)


def solution(mesh):
    placed = (
        P(("dp", "seq"), None),
        P(("dp", "seq"), None),
        P(("dp", "seq"), None),
        P(("dp", "seq"), None),
        P(),
        P("dp"),
        P(),
    )
    return jax.shard_map(
        local,
        mesh=mesh,
        in_specs=placed,
        out_specs=(
            P(("dp", "seq"), None),
            P(("dp", "seq"), None),
            P(("dp", "seq"), None),
            P(("dp", "seq"), None),
            P(("dp", "seq"), None),
        ),
        check_vma=False,
    )
```

profile of v0, /device:TPU:56, one launch (start us, length us, event | category | flops | bytes accessed | tf_op | source)
XLA Modules:
  0.0 1535.7 jit_solution(6381272670484574948)
XLA Ops:
  11.7 1.6 reshape_reshape.28
  13.2 1.6 select_reduce_fusion.1
  18.2 3.2 collective-permute-start
  22.1 1.6 reshape_reshape.29
  24.3 1.6 reshape_reshape.31
  28.2 2.6 collective-permute-start.3
  35.6 4.2 collective-permute-start.4
  40.0 2.7 collective-permute-done.4
  42.7 4.3 collective-permute-start.5
  48.1 4.1 collective-permute-start.1
  52.9 6.1 collective-permute-start.6
  59.8 2.2 collective-permute-start.2
  68.1 1.9 maximum_select_fusion.3
  70.0 10.4 collective-permute-start.7
  80.5 1.3 maximum_select_fusion
  88.8 1.5 maximum_select_fusion.1
  95.7 1.4 convolution_bitcast_fusion.12
  98.2 2.4 copy.273
  100.5 2.5 fusion.15
  106.0 1.3 fusion.5
  112.6 1.9 convolution_bitcast_fusion
  117.2 1.4 copy.297
  119.9 1.4 copy.296
  122.1 11.9 collective-permute-start.8
  135.4 1.4 copy.306
  136.7 2.4 stack.45
  139.2 2.1 copy.305
  141.3 2.0 fusion.43
  143.3 7.2 collective-permute-start.11
  151.6 2.4 copy.285
  154.0 1.9 broadcast_in_dim.403
  155.9 2.3 copy.292
  158.3 2.0 fusion.2
  162.1 1.7 copy.315
  163.9 2.2 convolution_convert_fusion.1
  167.3 4.6 collective-permute-start.12
  173.1 2.2 collective-permute-start.9
  175.3 6.3 collective-permute-done.12
  181.7 2.0 collective-permute-start.13
  183.6 4.1 collective-permute-done.9
  187.9 1.9 collective-permute-start.10
  189.9 4.0 collective-permute-start.14
  194.4 3.0 collective-permute-done.14
  197.4 3.3 collective-permute-start.15
  204.5 2.1 fusion.16
  206.6 1.8 copy.316
  210.6 1.8 fusion.17
  213.2 1313.5 %all-reduce.3.cloned.1.call-done = f32[768,768]{0,1:T(8,128)} async-done(((f32[768,768]{0,1:T(8,128)}), f32[768,768]{0,1:T(8,128)}) %all-reduce.3.cloned.1.call-update) | async-done | bytes 2359312
  (292 shorter events, 66.1 us)
Async XLA Ops:
  7.2 3.2 copy-start.12
  7.2 3.8 copy-start.13
  7.2 1519.6 %all-reduce.3.cloned.1.call-start = ((), (), s32[]{:S(2)}) async-start(), calls=%async_computation | async-start | bytes 4718592
  8.5 4.8 copy-start.65
  14.8 8.9 copy-start.14
  18.2 28.7 %collective-permute-start = (bf16[2,32,768]{2,1,0:T(8,128)(2,1)}, bf16[2,32,768]{2,1,0:T(8,128)(2,1)}, u32[]{:S(2)}, u32[]{:S(2)}) collective-permute-start(bf16[2,32,768]{2,1,0:T(8,128)(2,1)} %constant_dynamic-update-slice_fusion), channel_id=1, source_target_pairs={{0,1},{1,0},{2,3},{3,2},{4,5},{5,4},{6,7},{7,6},{8,9},{9,8},{10,11... | collective-permute-start | bytes 294920 | tf_op jit(solution)/shard_map/ppermute | solution.py:17
  25.9 7.1 copy-start.58
  27.2 65.4 %copy-start.34 = (bf16[8,16,48]{2,1,0:T(8,128)(2,1)}, bf16[8,16,48]{2,1,0:T(8,128)(2,1)S(1)}, u32[]{:S(2)}) copy-start(bf16[8,16,48]{2,1,0:T(8,128)(2,1)S(1)} %get-tuple-element.33) | copy-start | bytes 36868
  28.2 7.4 collective-permute-start.3
  33.1 19.8 %copy-start.27 = (bf16[128,768]{0,1:T(8,128)(2,1)}, bf16[128,768]{0,1:T(8,128)(2,1)S(1)}, u32[]{:S(2)}) copy-start(bf16[128,768]{0,1:T(8,128)(2,1)S(1)} %copy.251) | copy-start | bytes 589828
  34.6 32.5 %copy-start.41 = (s32[128,16]{0,1:T(8,128)}, s32[128,16]{0,1:T(8,128)S(1)}, u32[]{:S(2)}) copy-start(s32[128,16]{0,1:T(8,128)S(1)} %convert_reduce_fusion.3) | copy-start | bytes 24580
  35.5 32.7 %copy-start.55 = (f32[16,128]{1,0:T(8,128)}, f32[16,128]{1,0:T(8,128)S(1)}, u32[]{:S(2)}) copy-start(f32[16,128]{1,0:T(8,128)S(1)} %get-tuple-element.62) | copy-start | bytes 24580
  35.5 49.2 %copy-start.2 = (f32[16,128,128]{1,2,0:T(8,128)}, f32[16,128,128]{1,2,0:T(8,128)S(1)}, u32[]{:S(2)}) copy-start(f32[16,128,128]{1,2,0:T(8,128)S(1)} %get-tuple-element.63) | copy-start | bytes 3145732
  35.5 27.4 %copy-start.15 = (bf16[128,768]{1,0:T(8,128)(2,1)S(1)}, bf16[128,768]{1,0:T(8,128)(2,1)}, u32[]{:S(2)}) copy-start(bf16[128,768]{1,0:T(8,128)(2,1)} %param.12) | copy-start | bytes 589828
  35.5 28.3 %copy-start.59 = (pred[16,16]{1,0:T(8,128)(4,1)S(1)}, pred[16,16]{1,0:T(8,128)(4,1)}, u32[]{:S(2)}) copy-start(pred[16,16]{1,0:T(8,128)(4,1)} %copy-done.58) | copy-start | bytes 772
  35.5 29.0 %copy-start.66 = (pred[4,16]{1,0:T(4,128)(4,1)S(1)}, pred[4,16]{1,0:T(4,128)(4,1)}, u32[]{:S(2)}) copy-start(pred[4,16]{1,0:T(4,128)(4,1)} %copy-done.65) | copy-start | bytes 196
  35.6 7.0 collective-permute-start.4
  40.0 46.9 %copy-start.32 = (s32[256,16]{0,1:T(8,128)}, s32[256,16]{0,1:T(8,128)S(1)}, u32[]{:S(2)}) copy-start(s32[256,16]{0,1:T(8,128)S(1)} %get-tuple-element.42) | copy-start | bytes 49156
  42.7 10.2 collective-permute-start.5
  48.1 11.7 collective-permute-start.1
  52.9 15.2 collective-permute-start.6
  59.8 20.7 %collective-permute-start.2 = (bf16[2,128,768]{2,1,0:T(8,128)(2,1)S(1)}, bf16[2,128,768]{2,1,0:T(8,128)(2,1)}, u32[]{:S(2)}, u32[]{:S(2)}) collective-permute-start(bf16[2,128,768]{2,1,0:T(8,128)(2,1)S(1)} %maximum_select_fusion.2), channel_id=1, source_target_pairs={{0,4},{1,5},{2,6},{3,7},{4,0},{5,1},{6,2},{7,3},{8,12},{9,13},{10,... | collective-permute-start | bytes 1179656 | tf_op jit(solution)/shard_map/ppermute | solution.py:17
  63.8 29.0 %copy-start.36 = (s32[16,8]{1,0:T(8,128)}, s32[16,8]{1,0:T(8,128)S(1)}, u32[]{:S(2)}) copy-start(s32[16,8]{1,0:T(8,128)S(1)} %copy.258) | copy-start | bytes 1540
  70.0 18.8 %collective-permute-start.7 = (bf16[2,128,768]{2,1,0:T(8,128)(2,1)}, bf16[2,128,768]{2,1,0:T(8,128)(2,1)}, u32[]{:S(2)}, u32[]{:S(2)}) collective-permute-start(bf16[2,128,768]{2,1,0:T(8,128)(2,1)} %maximum_select_fusion.3), channel_id=1, source_target_pairs={{0,16},{1,17},{2,18},{3,19},{4,20},{5,21},{6,22},{7,23},{8,24},{9,... | collective-permute-start | bytes 1179656 | tf_op jit(solution)/shard_map/ppermute | solution.py:17
  91.3 3.4 copy-start.18
  92.5 3.1 copy-start.5
  95.7 4.9 copy-start.3
  106.0 3.6 copy-start.64
  106.0 3.6 copy-start.63
  106.0 3.7 copy-start.37
  106.0 3.7 copy-start.39
  107.4 3.6 copy-start.7
  119.9 14.2 copy-start.9
  122.1 49.8 %collective-permute-start.8 = (bf16[2,128,768]{2,1,0:T(8,128)(2,1)}, bf16[2,128,768]{2,1,0:T(8,128)(2,1)}, u32[]{:S(2)}, u32[]{:S(2)}) collective-permute-start(bf16[2,128,768]{2,1,0:T(8,128)(2,1)} %fusion.42), channel_id=1, source_target_pairs={{0,4},{1,5},{2,6},{3,7},{4,0},{5,1},{6,2},{7,3},{8,12},{9,13},{10,... | collective-permute-start | bytes 1179656 | tf_op jit(solution)/shard_map/ppermute | solution.py:17
  141.3 9.3 copy-start.24
  143.3 22.9 %collective-permute-start.11 = (bf16[2,128,768]{2,1,0:T(8,128)(2,1)}, bf16[2,128,768]{2,1,0:T(8,128)(2,1)}, u32[]{:S(2)}, u32[]{:S(2)}) collective-permute-start(bf16[2,128,768]{2,1,0:T(8,128)(2,1)} %fusion.43), channel_id=1, source_target_pairs={{0,16},{1,17},{2,18},{3,19},{4,20},{5,21},{6,22},{7,23},{8,24},{9,... | collective-permute-start | bytes 1179656 | tf_op jit(solution)/shard_map/ppermute | solution.py:17
  154.0 4.3 copy-start.42
  154.0 4.3 copy-start.47
  167.3 14.3 collective-permute-start.12
  173.1 14.7 collective-permute-start.9
  181.7 8.1 collective-permute-start.13
  187.9 6.5 collective-permute-start.10
  189.9 7.5 collective-permute-start.14
  197.4 5.7 collective-permute-start.15
  206.6 4.0 copy-start.4
  206.6 4.0 copy-start.25
  206.6 4.0 copy-start.51
  206.6 4.0 copy-start.54
  (37 other events, 91.8 us)
Sparse Core Ops, SparseCore 0:
  164.0 1362.6 all-reduce.2
where the time goes:
time: 1540 us
  waiting for transfers between devices  1330 us (86%)
  starting transfers between devices  74.5 us (5%)
  local copies, waits for them, and re-layouts  68.3 us (4%)
  matrix products  24.5 us (2%)
  other arithmetic  21.2 us (1%)
  between operations  16 us (1%)
    unnamed x2, waiting for transfers between devices  1310 us
    ppermute x16, starting transfers between devices, from_partner(): return lax.ppermute(value, axis, pairs)  74.4 us
  transfers between devices with their start and end apart: 17, of which 9 were waited for; matrix products, arithmetic and copies ran while one was open for 4% of the time, Pallas kernels for 0%

commit v1 on v0

v1 whole, which is shorter than its diff:
```python
import jax
import jax.numpy as jnp
from jax import lax
from jax.experimental import pallas as pl
from jax.experimental.pallas import tpu as pltpu
from jax.sharding import PartitionSpec as P

HEADS = 16
DIM = 48
WIDTH = HEADS * DIM
ROWS = 128
TILES = WIDTH // 128
HALF = WIDTH // 2
RATE = (4, 16)
COUNT = (ROWS // 4, ROWS // 16)
SCALE = DIM**-0.5
HIDDEN = -1e30
F32 = jnp.float32
BF16 = jnp.bfloat16
MESH = pl.DeviceIdType.MESH


def matmul(a, b, contract):
    return lax.dot_general(a, b, ((contract[:1], contract[1:]), ((), ())), preferred_element_type=F32)


def iota(shape, axis):
    return lax.broadcasted_iota(jnp.int32, shape, axis)


def over_48(columns):
    return (columns * 1366) >> 16


def tile_span(first, width):
    return range(first // 128, (first + width - 1) // 128 + 1)


def take_window(tiles, first, width, place):
    at, off = first // 128, first % 128
    turn = (place - off) % 128
    near = tiles[at] if turn == 0 else pltpu.roll(tiles[at], turn, 1)
    if off + width <= 128:
        return near
    far = tiles[at + 1] if turn == 0 else pltpu.roll(tiles[at + 1], turn, 1)
    return jnp.where(iota(near.shape, 1) < place + 128 - off, near, far)


def put_windows(windows, width, place):
    tiles = [None] * TILES
    for index, window in enumerate(windows):
        first = index * width
        off = first % 128
        turn = (off - place) % 128
        turned = window if turn == 0 else pltpu.roll(window, turn, 1)
        for tile in tile_span(first, width):
            if tiles[tile] is None:
                tiles[tile] = turned
            else:
                columns = iota(window.shape, 1) + 128 * tile
                inside = (columns >= first) & (columns < first + width)
                tiles[tile] = jnp.where(inside, turned, tiles[tile])
    return tiles


def three_parts(value):
    high = value.astype(BF16).astype(F32)
    rest = value - high
    middle = rest.astype(BF16).astype(F32)
    return high, middle, rest - middle


def kernel(
    q_ref,
    k_ref,
    v_ref,
    cot_ref,
    weight_ref,
    length_ref,
    shift_ref,
    mixed_ref,
    dq_ref,
    dk_ref,
    dv_ref,
    dw_ref,
    source,
    send_two,
    recv_two,
    send_three,
    recv_three,
    out_send_two,
    out_recv_two,
    out_send_three,
    out_recv_three,
    stat_send_two,
    stat_recv_two,
    stat_send_three,
    stat_recv_three,
    grad_send_two,
    grad_recv_two,
    grad_send_three,
    grad_recv_three,
    cot_halves,
    att_halves,
    cot_all,
    att_all,
    part,
    z_send,
    z_recv,
    y_send,
    y_recv,
    scores_one,
    scores_two,
    scores_three,
    level_out,
    level_lse,
    lse_wide,
    delta_wide,
    totals,
    send_sems,
    recv_sems,
):
    rank = lax.axis_index("seq")
    x, z, y = rank // 32, (rank % 32) // 4, rank % 4
    x_high, x_low = x // 2, x % 2
    plane, mine_three = rank - rank % 32, rank % 32
    block, mine_two = rank - rank % 8, rank % 8
    has_head = mine_three % 2 == (mine_three // 4) % 2
    own_head = mine_three // 2

    def worker(head):
        return 2 * head + (head // 2) % 2

    barrier = pltpu.get_barrier_semaphore()

    def greet(device):
        pl.semaphore_signal(barrier, inc=1, device_id={"seq": device}, device_id_type=MESH)

    @pl.loop(1, 32)
    def _(step):
        greet(plane + (mine_three + step) % 32)

    @pl.loop(1, 4)
    def _(step):
        greet(((x + step) % 4) * 32 + mine_three)

    other_x = 2 * x_high + 1 - x_low

    @pl.loop(1, 4)
    def _(step):
        greet(other_x * 32 + z * 4 + (y + step) % 4)

    def push(from_ref, to_ref, index, device):
        pltpu.make_async_remote_copy(
            src_ref=from_ref,
            dst_ref=to_ref,
            send_sem=send_sems.at[index],
            recv_sem=recv_sems.at[index],
            device_id={"seq": device},
            device_id_type=MESH,
        ).start()

    def keep(from_ref, to_ref, index):
        pltpu.make_async_copy(from_ref, to_ref, recv_sems.at[index]).start()

    def arrived(ref, index):
        pltpu.make_async_copy(ref, ref, recv_sems.at[index]).wait()

    def left(ref, index):
        pltpu.make_async_copy(ref, ref, send_sems.at[index]).wait()

    d_attended = jnp.dot(cot_ref[...], weight_ref[...], preferred_element_type=F32).astype(BF16)
    for index, ref in enumerate((q_ref, k_ref, v_ref, None)):
        for tile in range(TILES):
            lanes = slice(128 * tile, 128 * tile + 128)
            value = d_attended[:, lanes] if ref is None else ref[:, lanes]
            source[index, tile] = value.astype(F32)
    cot_halves[0] = cot_ref[:, :HALF]
    cot_halves[1] = cot_ref[:, HALF:]

    def column_shift(level, tile):
        shape = (COUNT[level], 128)
        heads = over_48(iota(shape, 1) + 128 * tile)
        value = jnp.zeros(shape, jnp.int32)
        for head in range(HEADS):
            if tile in tile_span(head * DIM, DIM):
                value = jnp.where(heads == head, shift_ref[level, head], value)
        return value

    shifts = [[column_shift(level, tile) for tile in range(TILES)] for level in range(2)]

    def pick(view, level):
        tiles = []
        for tile in range(TILES):
            value = view[tile, pl.ds(0, COUNT[level], RATE[level]), :]
            for offset in range(1, RATE[level]):
                rows = view[tile, pl.ds(offset, COUNT[level], RATE[level]), :]
                value = jnp.where(shifts[level][tile] == offset, rows, value)
            tiles.append(value)
        return tiles

    def spread(view, level, tiles, add):
        for tile in range(TILES):
            for offset in range(RATE[level]):
                place = (tile, pl.ds(offset, COUNT[level], RATE[level]), slice(None))
                other = view[place] if add else HIDDEN
                value = tiles[tile] + other if add else tiles[tile]
                view[place] = jnp.where(shifts[level][tile] == offset, value, other)

    picked_three = [pick(source.at[index], 1) for index in range(4)]
    for head in range(HEADS):
        low = iota((8, 128), 1) < 64
        for half in range(2):
            near = take_window(picked_three[2 * half], head * DIM, DIM, 0)
            far = take_window(picked_three[2 * half + 1], head * DIM, DIM, 64)
            totals[0, 0, 8 * half : 8 * half + 8] = jnp.where(low, near, far)
        send_three[head] = totals[0, 0, 0:16].astype(BF16)
    for index in range(4):
        picked = pick(source.at[index], 0)
        for other in range(8):
            send_two[other, index] = take_window(picked, 96 * other, 96, 0).astype(BF16)

    pl.semaphore_wait(barrier, 37)

    @pl.loop(1, 8)
    def _(step):
        other = (mine_two + step) % 8
        push(send_two.at[other], recv_two.at[:, pl.ds(32 * mine_two, 32)], 0, block + other)

    keep(send_two.at[mine_two], recv_two.at[:, pl.ds(32 * mine_two, 32)], 0)

    @pl.loop(0, HEADS)
    def _(step):
        head = (own_head + step) % HEADS
        other = worker(head)

        @pl.when(other != mine_three)
        def _():
            push(send_three.at[head], recv_three.at[mine_three], 1, plane + other)

    @pl.when(has_head)
    def _():
        keep(send_three.at[own_head], recv_three.at[mine_three], 1)

    @pl.loop(1, 4)
    def _(step):
        other = (x + step) % 4
        push(cot_halves.at[other // 2], cot_all.at[x], 2, other * 32 + mine_three)

    keep(cot_halves.at[x_high], cot_all.at[x], 2)

    ends = []
    running = 0
    for index in range(8):
        running = running + length_ref[index]
        ends.append(running)

    def slide(positions):
        value = jnp.zeros(positions.shape, jnp.int32)
        for end in ends:
            value = value + jnp.where(positions >= end, 1, 0)
        return value

    def seen(count, first, stride):
        rows = slide(first + stride * iota((count, 128), 0))
        columns = slide(first + stride * iota((8, count), 1))[0:1]
        rows = jnp.concatenate([rows] * (count // 128), axis=1)
        return rows == jnp.broadcast_to(columns, (count, count))

    def lane_mask(shape, first, width):
        lanes = iota(shape, 1)
        return (lanes >= first) & (lanes < first + width)

    def masked(value, first, width):
        inside = lane_mask(value.shape, first, width)
        return jnp.where(inside, value.astype(F32), 0.0).astype(BF16)

    def window(head):
        span = tile_span(head * DIM, DIM)
        return slice(128 * span[0], 128 * (span[-1] + 1)), head * DIM - 128 * span[0], span

    visible_one = seen(ROWS, ROWS * rank, 1)
    outs, tops, sums = ([None] * TILES for _ in range(3))

    def merge(tiles, head, value, wide):
        _, first, span = window(head)
        for index, tile in enumerate(span):
            piece = value[:, 128 * index : 128 * index + 128] if wide else value
            piece = jnp.broadcast_to(piece, (ROWS, 128))
            if tiles[tile] is None:
                tiles[tile] = piece
            else:
                columns = iota((ROWS, 128), 1) + 128 * index
                inside = (columns >= first) & (columns < first + DIM)
                tiles[tile] = jnp.where(inside, piece, tiles[tile])

    for head in range(HEADS):
        lanes, first, span = window(head)
        scores = matmul(masked(q_ref[:, lanes], first, DIM), k_ref[:, lanes], (1, 1)) * SCALE
        scores = jnp.where(visible_one, scores, HIDDEN)
        scores_one[head] = scores
        top = jnp.max(scores, axis=1, keepdims=True)
        weights = jnp.exp(scores - top)
        total = jnp.sum(weights, axis=1, keepdims=True)
        out = matmul(weights.astype(BF16), v_ref[:, lanes], (1, 0))
        merge(outs, head, out, True)
        merge(tops, head, top, False)
        merge(sums, head, total, False)
    for tile in range(TILES):
        level_out[0, tile] = outs[tile] / sums[tile]
        level_lse[0, tile] = tops[tile] + jnp.log(sums[tile])

    def split_three():
        both = recv_three[...].astype(F32).reshape(32, 2, 8, 128)
        first = both[:, 0].reshape(256, 128)
        second = both[:, 1].reshape(256, 128)
        return first, second, pltpu.roll(first, 64, 1), pltpu.roll(second, 64, 1)

    def part_of(value, first):
        return jnp.where(lane_mask(value.shape, first, DIM), value, 0.0).astype(BF16)

    @pl.when(has_head)
    def _():
        arrived(recv_three, 1)
        first, second, first_turned, second_turned = split_three()
        scores = matmul(part_of(first, 0), first_turned.astype(BF16), (1, 1)) * SCALE
        visible = seen(256, 4096 * x + shift_ref[1, own_head], RATE[1])
        scores = jnp.where(visible, scores, HIDDEN)
        scores_three[...] = scores
        top = jnp.max(scores, axis=1, keepdims=True)
        weights = jnp.exp(scores - top)
        total = jnp.sum(weights, axis=1, keepdims=True)
        out = matmul(weights.astype(BF16), second.astype(BF16), (1, 0)) / total
        lse = jnp.broadcast_to(top + jnp.log(total), (256, 128))
        out = jnp.where(iota((256, 128), 1) < 64, out, lse)
        out_send_three[...] = out.reshape(32, 8, 128)

        @pl.loop(1, 32)
        def _(step):
            other = (mine_three + step) % 32
            push(out_send_three.at[other], out_recv_three.at[own_head], 3, plane + other)

        keep(out_send_three.at[mine_three], out_recv_three.at[own_head], 3)

    arrived(recv_two, 0)
    out_two, lse_two = None, None
    lanes_two = iota((256, 128), 1)
    for member in range(2):
        head = 2 * mine_two + member
        scores = matmul(masked(recv_two[0], DIM * member, DIM), recv_two[1], (1, 1)) * SCALE
        visible = seen(256, ROWS * block + shift_ref[0, head], RATE[0])
        scores = jnp.where(visible, scores, HIDDEN)
        scores_two[member] = scores
        top = jnp.max(scores, axis=1, keepdims=True)
        weights = jnp.exp(scores - top)
        total = jnp.sum(weights, axis=1, keepdims=True)
        out = matmul(weights.astype(BF16), recv_two[2], (1, 0)) / total
        lse = jnp.broadcast_to(top + jnp.log(total), (256, 128))
        out_two = out if member == 0 else jnp.where(lanes_two < DIM, out_two, out)
        lse_two = lse if member == 0 else jnp.where(lanes_two < 112, lse_two, lse)
    high, middle, low = three_parts(lse_two)
    turn = lanes_two % 16
    lse_two = jnp.where(turn == 0, high, jnp.where(turn == 1, middle, jnp.where(turn == 2, low, 0.0)))
    out_send_two[...] = jnp.where(lanes_two < 96, out_two, lse_two).astype(BF16)

    @pl.loop(1, 8)
    def _(step):
        other = (mine_two + step) % 8
        push(out_send_two.at[pl.ds(32 * other, 32)], out_recv_two.at[mine_two], 4, block + other)

    keep(out_send_two.at[pl.ds(32 * mine_two, 32)], out_recv_two.at[mine_two], 4)

    arrived(out_recv_three, 3)
    out_three = put_windows([out_recv_three[head] for head in range(HEADS)], DIM, 0)
    lse_three = put_windows([out_recv_three[head] for head in range(HEADS)], DIM, 64)
    spread(level_out.at[2], 1, out_three, False)
    spread(level_lse.at[2], 1, lse_three, False)
    arrived(out_recv_two, 4)
    row, column = iota((128, 128), 0), iota((128, 128), 1)
    widen = ((row >= 96) & (row < 99) & (column < DIM)) | (
        (row >= 112) & (row < 115) & (column >= DIM) & (column < 96)
    )
    widen = jnp.where(widen, 1.0, 0.0).astype(BF16)
    all_two = out_recv_two[...].reshape(256, 128)
    lse_all = matmul(all_two, widen, (1, 0)).reshape(8, 32, 128)
    out_all = all_two.astype(F32).reshape(8, 32, 128)
    spread(level_out.at[1], 0, put_windows([out_all[i] for i in range(8)], 96, 0), False)
    spread(level_lse.at[1], 0, put_windows([lse_all[i] for i in range(8)], 96, 0), False)
    for tile in range(TILES):
        levels = [level_lse[level, tile] for level in range(3)]
        best = jnp.maximum(jnp.maximum(levels[0], levels[1]), levels[2])
        mass = sum(jnp.exp(level - best) for level in levels)
        lse = best + jnp.log(mass)
        lse_wide[tile] = lse
        combined = jnp.zeros((ROWS, 128), F32)
        for level in range(3):
            share = jnp.exp(levels[level] - lse)
            combined = combined + jnp.where(share > 0, share * level_out[level, tile], 0.0)
        half, place = tile // 3, 128 * (tile % 3)
        att_halves[half, :, place : place + 128] = combined.astype(BF16)

    @pl.loop(1, 4)
    def _(step):
        other = (x + step) % 4
        push(att_halves.at[other % 2], att_all.at[x], 5, other * 32 + mine_three)

    keep(att_halves.at[x_low], att_all.at[x], 5)

    same_head = over_48(iota((HALF, HALF), 0)) == over_48(iota((HALF, HALF), 1))
    same_head = jnp.where(same_head, 1.0, 0.0).astype(BF16)
    for half in range(2):
        product = jnp.concatenate([source[3, 3 * half + tile] for tile in range(3)], axis=1)
        product = product * att_halves[half].astype(F32)
        high, middle, low = three_parts(product)
        summed = matmul(high.astype(BF16), same_head, (1, 0))
        summed = summed + matmul(middle.astype(BF16), same_head, (1, 0))
        for tile in range(3):
            delta_wide[3 * half + tile] = summed[:, 128 * tile : 128 * tile + 128]

    picked_lse, picked_delta = pick(lse_wide, 1), pick(delta_wide, 1)
    for head in range(HEADS):
        near = take_window(picked_lse, head * DIM, DIM, 0)
        far = take_window(picked_delta, head * DIM, DIM, 64)
        stat_send_three[head] = jnp.where(iota((8, 128), 1) < 64, near, far)
    picked_lse, picked_delta = pick(lse_wide, 0), pick(delta_wide, 0)
    coded = []
    for tile in range(TILES):
        columns = iota((32, 128), 1) + 128 * tile
        turn = (columns - DIM * over_48(columns)) >> 3
        value = jnp.zeros((32, 128), F32)
        pieces = three_parts(picked_lse[tile]) + three_parts(picked_delta[tile])
        for index, piece in enumerate(pieces):
            value = jnp.where(turn == index, piece, value)
        coded.append(value)
    for other in range(8):
        stat_send_two[other] = take_window(coded, 96 * other, 96, 0).astype(BF16)

    @pl.loop(1, 8)
    def _(step):
        other = (mine_two + step) % 8
        push(stat_send_two.at[other], stat_recv_two.at[pl.ds(32 * mine_two, 32)], 6, block + other)

    keep(stat_send_two.at[mine_two], stat_recv_two.at[pl.ds(32 * mine_two, 32)], 6)

    @pl.loop(0, HEADS)
    def _(step):
        head = (own_head + step) % HEADS
        other = worker(head)

        @pl.when(other != mine_three)
        def _():
            push(stat_send_three.at[head], stat_recv_three.at[mine_three], 7, plane + other)

    @pl.when(has_head)
    def _():
        keep(stat_send_three.at[own_head], stat_recv_three.at[mine_three], 7)

    attended = jnp.concatenate([att_halves[0], att_halves[1]], axis=1)
    mixed_ref[...] = matmul(attended, weight_ref[...], (1, 1)).astype(BF16)

    sums_q, sums_k, sums_v = ([None] * TILES for _ in range(3))
    for head in range(HEADS):
        lanes, first, span = window(head)
        place = slice(first, first + 1) if first < 128 else slice(first - 128, first - 127)
        lse = lse_wide[span[0]][:, place]
        delta = delta_wide[span[0]][:, place]
        grad = jnp.concatenate([source[3, tile] for tile in span], axis=1)
        grad_low = grad.astype(BF16)
        grad_head = part_of(grad, first)
        prob = jnp.exp(scores_one[head] - lse)
        dprob = matmul(grad_head, v_ref[:, lanes], (1, 1))
        dscore = (prob * (dprob - delta) * SCALE).astype(BF16)
        merge(sums_q, head, matmul(dscore, k_ref[:, lanes], (1, 0)), True)
        merge(sums_k, head, matmul(dscore, q_ref[:, lanes], (0, 0)), True)
        merge(sums_v, head, matmul(prob.astype(BF16), grad_low, (0, 0)), True)
    for tile in range(TILES):
        totals[0, tile] = sums_q[tile]
        totals[1, tile] = sums_k[tile]
        totals[2, tile] = sums_v[tile]

    @pl.when(has_head)
    def _():
        arrived(stat_recv_three, 7)
        first, second, first_turned, second_turned = split_three()
        stats = stat_recv_three[...].reshape(256, 128)
        prob = jnp.exp(scores_three[...] - stats[:, 0:1])
        dprob = matmul(part_of(second_turned, 0), second.astype(BF16), (1, 1))
        dscore = (prob * (dprob - stats[:, 64:65]) * SCALE).astype(BF16)
        grad_qk = matmul(dscore, part_of(first_turned, 0), (1, 0))
        grad_qk = grad_qk + matmul(dscore, part_of(first_turned, 64), (0, 0))
        grad_v = matmul(prob.astype(BF16), part_of(second_turned, 0), (0, 0))
        grads = jnp.concatenate([grad_qk.reshape(32, 8, 128), grad_v.reshape(32, 8, 128)], axis=1)
        grad_send_three[...] = grads.astype(BF16)

        @pl.loop(1, 32)
        def _(step):
            other = (mine_three + step) % 32
            push(grad_send_three.at[other], grad_recv_three.at[own_head], 8, plane + other)

        keep(grad_send_three.at[mine_three], grad_recv_three.at[own_head], 8)

    arrived(stat_recv_two, 6)
    row = iota((128, 256), 0)
    stats = stat_recv_two[...]
    grads = [None] * 3
    for member in range(2):

        def gathered(first):
            hit = (row == first) | (row == first + 8) | (row == first + 16)
            return matmul(stats, jnp.where(hit, 1.0, 0.0).astype(BF16), (1, 0))

        prob = jnp.exp(scores_two[member] - gathered(DIM * member))
        dprob = matmul(masked(recv_two[3], DIM * member, DIM), recv_two[2], (1, 1))
        dscore = (prob * (dprob - gathered(DIM * member + 24)) * SCALE).astype(BF16)
        news = (
            matmul(dscore, recv_two[1], (1, 0)),
            matmul(dscore, recv_two[0], (0, 0)),
            matmul(prob.astype(BF16), recv_two[3], (0, 0)),
        )
        for index, new in enumerate(news):
            old = grads[index]
            grads[index] = new if member == 0 else jnp.where(lanes_two < DIM, old, new)
    for index in range(3):
        grad_send_two[index] = grads[index].astype(BF16)

    @pl.loop(1, 8)
    def _(step):
        other = (mine_two + step) % 8
        push(grad_send_two.at[:, pl.ds(32 * other, 32)], grad_recv_two.at[mine_two], 9, block + other)

    keep(grad_send_two.at[:, pl.ds(32 * mine_two, 32)], grad_recv_two.at[mine_two], 9)

    arrived(cot_all, 2)
    arrived(att_all, 5)
    part[...] = matmul(
        cot_all[...].reshape(4 * ROWS, HALF), att_all[...].reshape(4 * ROWS, HALF), (0, 0)
    )
    for other in range(8):
        rows = jnp.concatenate(
            [part[24 * other : 24 * other + 24], part[192 + 24 * other : 216 + 24 * other]], axis=0
        )
        z_send[other] = rows.astype(BF16)

    @pl.loop(1, 8)
    def _(step):
        other = (z + step) % 8
        push(z_send.at[other], z_recv.at[z], 10, plane + 4 * other + y)

    keep(z_send.at[z], z_recv.at[z], 10)

    arrived(grad_recv_three, 8)
    received = grad_recv_three[...].astype(F32)
    for index, (place, rows) in enumerate(((0, slice(0, 8)), (64, slice(0, 8)), (0, slice(8, 16)))):
        tiles = put_windows([received[head, rows] for head in range(HEADS)], DIM, place)
        spread(totals.at[index], 1, tiles, True)
    arrived(grad_recv_two, 9)
    for index, out_ref in enumerate((dq_ref, dk_ref, dv_ref)):
        windows = [grad_recv_two[other, index].astype(F32) for other in range(8)]
        spread(totals.at[index], 0, put_windows(windows, 96, 0), True)
        for tile in range(TILES):
            out_ref[:, 128 * tile : 128 * tile + 128] = totals[index, tile].astype(BF16)

    arrived(z_recv, 10)
    rows = z_recv[0].astype(F32)
    for other in range(1, 8):
        rows = rows + z_recv[other].astype(F32)
    part[0:48] = rows
    for low in range(2):
        for other in range(4):
            start = 24 * low + 6 * other
            y_send[low, other, 0:6] = part[start : start + 6]
            y_send[low, other, 6:8] = jnp.zeros((2, HALF), F32)

    @pl.loop(1, 8)
    def _(step):
        other = (4 * x_low + y + step) % 8
        low, high = other // 4, other % 4
        device = (2 * x_high + low) * 32 + 4 * z + high
        push(y_send.at[low, high], y_recv.at[x_low, y], 11, device)

    keep(y_send.at[x_low, y], y_recv.at[x_low, y], 11)
    arrived(y_recv, 11)
    for low in range(2):
        rows = (y_recv[low, 0] + y_recv[low, 1]) + (y_recv[low, 2] + y_recv[low, 3])
        dw_ref[:, HALF * low : HALF * low + HALF] = rows[0:6] * (16384**-0.5)

    left(send_two.at[0:7], 0)
    left(cot_all.at[0:3], 2)
    left(out_send_two.at[0:224], 4)
    left(att_all.at[0:3], 5)
    left(stat_send_two.at[0:7], 6)
    left(grad_recv_two.at[0:7], 9)
    left(z_send.at[0:7], 10)
    left(y_send.at[0:1], 11)
    left(y_send.at[0, 0:3], 11)

    @pl.when(has_head)
    def _():
        left(send_three.at[0:15], 1)
        left(stat_send_three.at[0:15], 7)
        left(out_send_three.at[0:31], 3)
        left(grad_send_three.at[0:31], 8)

    @pl.when(jnp.logical_not(has_head))
    def _():
        left(send_three, 1)
        left(stat_send_three, 7)


def local(queries, keys, values, cotangent, out_weight, slide_lengths, head_dilation_shifts):
    vmem = pl.BlockSpec(memory_space=pltpu.VMEM)
    smem = pl.BlockSpec(memory_space=pltpu.SMEM)
    wide = jax.ShapeDtypeStruct((ROWS, WIDTH), BF16)
    scratch = [
        ((4, TILES, ROWS, 128), F32),
        ((8, 4, 32, 128), BF16),
        ((4, 256, 128), BF16),
        ((16, 16, 128), BF16),
        ((32, 16, 128), BF16),
        ((256, 128), BF16),
        ((8, 32, 128), BF16),
        ((32, 8, 128), F32),
        ((16, 8, 128), F32),
        ((8, 32, 128), BF16),
        ((256, 128), BF16),
        ((16, 8, 128), F32),
        ((32, 8, 128), F32),
        ((3, 256, 128), BF16),
        ((8, 3, 32, 128), BF16),
        ((32, 16, 128), BF16),
        ((16, 16, 128), BF16),
        ((2, ROWS, HALF), BF16),
        ((2, ROWS, HALF), BF16),
        ((4, ROWS, HALF), BF16),
        ((4, ROWS, HALF), BF16),
        ((HALF, HALF), F32),
        ((8, 48, HALF), BF16),
        ((8, 48, HALF), BF16),
        ((2, 4, 8, HALF), F32),
        ((2, 4, 8, HALF), F32),
        ((HEADS, ROWS, ROWS), F32),
        ((2, 256, 256), F32),
        ((256, 256), F32),
        ((3, TILES, ROWS, 128), F32),
        ((3, TILES, ROWS, 128), F32),
        ((TILES, ROWS, 128), F32),
        ((TILES, ROWS, 128), F32),
        ((3, TILES, ROWS, 128), F32),
    ]
    return pl.pallas_call(
        kernel,
        out_shape=(wide, wide, wide, wide, jax.ShapeDtypeStruct((WIDTH // 128, WIDTH), F32)),
        in_specs=[vmem] * 5 + [smem] * 2,
        out_specs=(vmem,) * 5,
        scratch_shapes=[pltpu.VMEM(shape, dtype) for shape, dtype in scratch]
        + [pltpu.SemaphoreType.DMA((12,)), pltpu.SemaphoreType.DMA((12,))],
        compiler_params=pltpu.CompilerParams(
            collective_id=0, has_side_effects=True, vmem_limit_bytes=48 * 1024 * 1024
        ),
        name="dilated_attention",
    )(queries, keys, values, cotangent, out_weight, slide_lengths, head_dilation_shifts)


def solution(mesh):
    rows = P(("dp", "seq"), None)
    return jax.shard_map(
        local,
        mesh=mesh,
        in_specs=(rows, rows, rows, rows, P(), P("dp"), P()),
        out_specs=(rows,) * 5,
        check_vma=False,
    )
```

time: 1540 us -> 66.2 us (0.04)
  waiting for transfers between devices: 1330 us -> 0 us
  starting transfers between devices: 74.5 us -> 0 us
  local copies, waits for them, and re-layouts: 68.3 us -> 9.62 us
  Pallas kernels: 0 us -> 55.6 us
  matrix products: 24.5 us -> 0 us
  other arithmetic: 21.2 us -> 0 us
    unnamed x2 -> x0, waiting for transfers between devices: 1310 us -> none
    ppermute x16 -> x0, starting transfers between devices: 74.4 us -> none  [from_partner(): return lax.ppermute(value, axis, pairs)]
    pallas_call x0 -> x1, Pallas kernels: none -> 55.6 us  [local(): pl.pallas_call(kernel, out_shape=(wide, wide, wide, wide, jax.ShapeDtypeS...]
    dot_general x21 -> x0, matrix products: 24.5 us -> none  [the longest x3 4.49 us: attend_back(): jnp.einsum('hqk,qhd->khd', dscores, query_rows, preferred_element_type=jn...]
    another operation x22 -> x0, local copies, waits for them, and re-layouts: 24.1 us -> none  [the longest x8 12.5 us: local(): returning.append(jnp.stack([grad_k, grad_v]).reshape(2, -1, width))]
    broadcast_in_dim x32 -> x0, local copies, waits for them, and re-layouts: 20.9 us -> none  [spread(): wide = jnp.where(chosen[None], selected[:, None], fill)]
    ppermute x16 -> x0, waiting for transfers between devices: 17.7 us -> none  [from_partner(): return lax.ppermute(value, axis, pairs)]
  transfers between devices with their start and end apart: 17 -> 0, of which waited for: 9 -> 0; matrix products, arithmetic and copies ran while one was open for 4% -> 0% of each run, Pallas kernels for 0% -> 0%
where the time goes in v1:
time: 66.2 us; the launch traced here: 65.9 us
  Pallas kernels  55.6 us (84%)
  local copies, waits for them, and re-layouts  9.62 us (15%)
    pallas_call x1, Pallas kernels, local(): pl.pallas_call(kernel, out_shape=(wide, wide, wide, wide, jax.ShapeDtypeS...  55.6 us
    unnamed x19, local copies, waits for them, and re-layouts  9.62 us

profile of v1, /device:TPU:56, one launch (start us, length us, event | category | flops | bytes accessed | tf_op | source)
XLA Modules:
  0.0 65.9 jit_solution(16148127131029237659)
XLA Ops:
  0.6 0.0 copy-start
  0.6 1.3 %copy-done = bf16[768,768]{1,0:T(8,128)(2,1)S(1)} copy-done((bf16[768,768]{1,0:T(8,128)(2,1)S(1)}, bf16[768,768]{1,0:T(8,128)(2,1)}, u32[]{:S(2)}) %copy-start) | copy-done | bytes 1179672
  1.9 0.0 copy-start.1
  1.9 0.9 %copy-done.1 = bf16[128,768]{1,0:T(8,128)(2,1)S(1)} copy-done((bf16[128,768]{1,0:T(8,128)(2,1)S(1)}, bf16[128,768]{1,0:T(8,128)(2,1)}, u32[]{:S(2)}) %copy-start.1) | copy-done | bytes 196632
  2.8 0.0 copy-start.2
  2.8 0.9 %copy-done.2 = bf16[128,768]{1,0:T(8,128)(2,1)S(1)} copy-done((bf16[128,768]{1,0:T(8,128)(2,1)S(1)}, bf16[128,768]{1,0:T(8,128)(2,1)}, u32[]{:S(2)}) %copy-start.2) | copy-done | bytes 196632
  3.8 0.0 copy-start.3
  3.8 0.9 %copy-done.3 = bf16[128,768]{1,0:T(8,128)(2,1)S(1)} copy-done((bf16[128,768]{1,0:T(8,128)(2,1)S(1)}, bf16[128,768]{1,0:T(8,128)(2,1)}, u32[]{:S(2)}) %copy-start.3) | copy-done | bytes 196632
  4.7 0.0 copy-start.4
  4.7 0.9 %copy-done.4 = bf16[128,768]{1,0:T(8,128)(2,1)S(1)} copy-done((bf16[128,768]{1,0:T(8,128)(2,1)S(1)}, bf16[128,768]{1,0:T(8,128)(2,1)}, u32[]{:S(2)}) %copy-start.4) | copy-done | bytes 196632
  5.6 0.0 copy-start.5
  5.6 0.7 %copy-done.5 = s32[2,16]{1,0:T(2,128)S(1)} copy-done((s32[2,16]{1,0:T(2,128)S(1)}, s32[2,16]{1,0:T(2,128)}, u32[]{:S(2)}) %copy-start.5) | copy-done | bytes 152
  6.3 0.0 copy-start.6
  6.3 0.7 copy-done.6
  7.0 55.6 %dilated_attention.1 = (bf16[128,768]{1,0:T(8,128)(2,1)S(1)}, bf16[128,768]{1,0:T(8,128)(2,1)S(1)}, bf16[128,768]{1,0:T(8,128)(2,1)S(1)}, bf16[128,768]{1,0:T(8,128)(2,1)S(1)}, f32[6,768]{1,0:T(8,128)S(1)}) custom-call(bf16[128,768]{1,0:T(8,128)(2,1)S(1)} %copy-done.1, bf16[128,768]{1,0:T(8,128)(2,1)S(1)} %copy-done.2, bf16[128,768]{1,0:T(8,128)(2,1)S(1)} %copy-done.3, ...), custom_call_target="tpu_custom_call" | custom-call | tf_op jit(solution)/shard_map/dilated_attention/pallas_call | solution.py:650
  62.6 0.7 %copy.17 = bf16[128,768]{1,0:T(8,128)(2,1)} copy(bf16[128,768]{1,0:T(8,128)(2,1)S(1)} %get-tuple-element.10) | data formatting | bytes 393216
  63.3 0.7 %copy.18 = bf16[128,768]{1,0:T(8,128)(2,1)} copy(bf16[128,768]{1,0:T(8,128)(2,1)S(1)} %get-tuple-element.11) | data formatting | bytes 393216
  64.0 0.7 %copy.19 = bf16[128,768]{1,0:T(8,128)(2,1)} copy(bf16[128,768]{1,0:T(8,128)(2,1)S(1)} %get-tuple-element.12) | data formatting | bytes 393216
  64.6 0.7 %copy.20 = bf16[128,768]{1,0:T(8,128)(2,1)} copy(bf16[128,768]{1,0:T(8,128)(2,1)S(1)} %get-tuple-element.13) | data formatting | bytes 393216
  65.3 0.6 copy.21
Async XLA Ops:
  0.6 1.3 %copy-start = (bf16[768,768]{1,0:T(8,128)(2,1)S(1)}, bf16[768,768]{1,0:T(8,128)(2,1)}, u32[]{:S(2)}) copy-start(bf16[768,768]{1,0:T(8,128)(2,1)} %weight_ref.1) | copy-start | bytes 3538948
  1.9 0.9 %copy-start.1 = (bf16[128,768]{1,0:T(8,128)(2,1)S(1)}, bf16[128,768]{1,0:T(8,128)(2,1)}, u32[]{:S(2)}) copy-start(bf16[128,768]{1,0:T(8,128)(2,1)} %q_ref.1) | copy-start | bytes 589828
  2.8 0.9 %copy-start.2 = (bf16[128,768]{1,0:T(8,128)(2,1)S(1)}, bf16[128,768]{1,0:T(8,128)(2,1)}, u32[]{:S(2)}) copy-start(bf16[128,768]{1,0:T(8,128)(2,1)} %k_ref.1) | copy-start | bytes 589828
  3.8 0.9 %copy-start.3 = (bf16[128,768]{1,0:T(8,128)(2,1)S(1)}, bf16[128,768]{1,0:T(8,128)(2,1)}, u32[]{:S(2)}) copy-start(bf16[128,768]{1,0:T(8,128)(2,1)} %v_ref.1) | copy-start | bytes 589828
  4.7 0.9 %copy-start.4 = (bf16[128,768]{1,0:T(8,128)(2,1)S(1)}, bf16[128,768]{1,0:T(8,128)(2,1)}, u32[]{:S(2)}) copy-start(bf16[128,768]{1,0:T(8,128)(2,1)} %cot_ref.1) | copy-start | bytes 589828
  5.6 0.7 %copy-start.5 = (s32[2,16]{1,0:T(2,128)S(1)}, s32[2,16]{1,0:T(2,128)}, u32[]{:S(2)}) copy-start(s32[2,16]{1,0:T(2,128)} %shift_ref.1) | copy-start | bytes 388
  6.3 0.7 copy-start.6

commit v2 on v1

--- a/solution.py
+++ b/solution.py
@@ -15,6 +15,8 @@
 COUNT = (ROWS // 4, ROWS // 16)
 SCALE = DIM**-0.5
 HIDDEN = -1e30
+EARLY = 8
+VMEM = 60 * 1024 * 1024
 F32 = jnp.float32
 BF16 = jnp.bfloat16
 MESH = pl.DeviceIdType.MESH
@@ -71,6 +73,23 @@
 
 
 def kernel(
+    q_far,
+    k_far,
+    v_far,
+    cot_far,
+    weight_far,
+    length_far,
+    shift_far,
+    mixed_far,
+    dq_far,
+    dk_far,
+    dv_far,
+    dw_far,
+    mixed_ref,
+    dq_ref,
+    dk_ref,
+    dv_ref,
+    dw_ref,
     q_ref,
     k_ref,
     v_ref,
@@ -78,14 +97,11 @@
     weight_ref,
     length_ref,
     shift_ref,
-    mixed_ref,
-    dq_ref,
-    dk_ref,
-    dv_ref,
-    dw_ref,
     source,
     send_two,
     recv_two,
+    d_send_two,
+    d_recv_two,
     send_three,
     recv_three,
     out_send_two,
@@ -119,7 +135,30 @@
     totals,
     send_sems,
     recv_sems,
+    in_sems,
+    out_sems,
 ):
+    pairs = (
+        (shift_far, shift_ref),
+        (q_far, q_ref),
+        (k_far, k_ref),
+        (v_far, v_ref),
+        (cot_far, cot_ref),
+        (weight_far, weight_ref),
+        (length_far, length_ref),
+    )
+    incoming = [pltpu.make_async_copy(*pair, in_sems.at[index]) for index, pair in enumerate(pairs)]
+    for copy in incoming:
+        copy.start()
+    pairs = (
+        (mixed_ref, mixed_far),
+        (dq_ref, dq_far),
+        (dk_ref, dk_far),
+        (dv_ref, dv_far),
+        (dw_ref, dw_far),
+    )
+    outgoing = [pltpu.make_async_copy(*pair, out_sems.at[index]) for index, pair in enumerate(pairs)]
+
     rank = lax.axis_index("seq")
     x, z, y = rank // 32, (rank % 32) // 4, rank % 4
     x_high, x_low = x // 2, x % 2
@@ -169,14 +208,11 @@
     def left(ref, index):
         pltpu.make_async_copy(ref, ref, send_sems.at[index]).wait()
 
-    d_attended = jnp.dot(cot_ref[...], weight_ref[...], preferred_element_type=F32).astype(BF16)
-    for index, ref in enumerate((q_ref, k_ref, v_ref, None)):
+    for index in range(4):
+        incoming[index].wait()
+    for index, ref in enumerate((q_ref, k_ref, v_ref)):
         for tile in range(TILES):
-            lanes = slice(128 * tile, 128 * tile + 128)
-            value = d_attended[:, lanes] if ref is None else ref[:, lanes]
-            source[index, tile] = value.astype(F32)
-    cot_halves[0] = cot_ref[:, :HALF]
-    cot_halves[1] = cot_ref[:, HALF:]
+            source[index, tile] = ref[:, 128 * tile : 128 * tile + 128].astype(F32)
 
     def column_shift(level, tile):
         shape = (COUNT[level], 128)
@@ -207,21 +243,35 @@
                 value = tiles[tile] + other if add else tiles[tile]
                 view[place] = jnp.where(shifts[level][tile] == offset, value, other)
 
-    picked_three = [pick(source.at[index], 1) for index in range(4)]
+    picked_three = [pick(source.at[index], 1) for index in range(3)]
     for head in range(HEADS):
         low = iota((8, 128), 1) < 64
-        for half in range(2):
-            near = take_window(picked_three[2 * half], head * DIM, DIM, 0)
-            far = take_window(picked_three[2 * half + 1], head * DIM, DIM, 64)
-            totals[0, 0, 8 * half : 8 * half + 8] = jnp.where(low, near, far)
+        near = take_window(picked_three[0], head * DIM, DIM, 0)
+        far = take_window(picked_three[1], head * DIM, DIM, 64)
+        totals[0, 0, 0:8] = jnp.where(low, near, far)
+        totals[0, 0, 8:16] = take_window(picked_three[2], head * DIM, DIM, 0)
         send_three[head] = totals[0, 0, 0:16].astype(BF16)
-    for index in range(4):
+
+    pl.semaphore_wait(barrier, 37)
+
+    @pl.loop(0, HEADS)
+    def _(step):
+        head = (own_head + step) % HEADS
+        other = worker(head)
+
+        @pl.when(other != mine_three)
+        def _():
+            push(send_three.at[head], recv_three.at[mine_three], 1, plane + other)
+
+    @pl.when(has_head)
+    def _():
+        keep(send_three.at[own_head], recv_three.at[mine_three], 1)
+
+    for index in range(3):
         picked = pick(source.at[index], 0)
         for other in range(8):
             send_two[other, index] = take_window(picked, 96 * other, 96, 0).astype(BF16)
 
-    pl.semaphore_wait(barrier, 37)
-
     @pl.loop(1, 8)
     def _(step):
         other = (mine_two + step) % 8
@@ -229,18 +279,10 @@
 
     keep(send_two.at[mine_two], recv_two.at[:, pl.ds(32 * mine_two, 32)], 0)
 
-    @pl.loop(0, HEADS)
-    def _(step):
-        head = (own_head + step) % HEADS
-        other = worker(head)
-
-        @pl.when(other != mine_three)
-        def _():
-            push(send_three.at[head], recv_three.at[mine_three], 1, plane + other)
-
-    @pl.when(has_head)
-    def _():
-        keep(send_three.at[own_head], recv_three.at[mine_three], 1)
+    for index in range(4, 7):
+        incoming[index].wait()
+    cot_halves[0] = cot_ref[:, :HALF]
+    cot_halves[1] = cot_ref[:, HALF:]
 
     @pl.loop(1, 4)
     def _(step):
@@ -248,6 +290,19 @@
         push(cot_halves.at[other // 2], cot_all.at[x], 2, other * 32 + mine_three)
 
     keep(cot_halves.at[x_high], cot_all.at[x], 2)
+    d_attended = jnp.dot(cot_ref[...], weight_ref[...], preferred_element_type=F32).astype(BF16)
+    for tile in range(TILES):
+        source[3, tile] = d_attended[:, 128 * tile : 128 * tile + 128].astype(F32)
+    picked = pick(source.at[3], 0)
+    for other in range(8):
+        d_send_two[other] = take_window(picked, 96 * other, 96, 0).astype(BF16)
+
+    @pl.loop(1, 8)
+    def _(step):
+        other = (mine_two + step) % 8
+        push(d_send_two.at[other], d_recv_two.at[pl.ds(32 * mine_two, 32)], 12, block + other)
+
+    keep(d_send_two.at[mine_two], d_recv_two.at[pl.ds(32 * mine_two, 32)], 12)
 
     ends = []
     running = 0
@@ -313,8 +368,7 @@
     def split_three():
         both = recv_three[...].astype(F32).reshape(32, 2, 8, 128)
         first = both[:, 0].reshape(256, 128)
-        second = both[:, 1].reshape(256, 128)
-        return first, second, pltpu.roll(first, 64, 1), pltpu.roll(second, 64, 1)
+        return first, pltpu.roll(first, 64, 1), both[:, 1].reshape(256, 128).astype(BF16)
 
     def part_of(value, first):
         return jnp.where(lane_mask(value.shape, first, DIM), value, 0.0).astype(BF16)
@@ -322,15 +376,15 @@
     @pl.when(has_head)
     def _():
         arrived(recv_three, 1)
-        first, second, first_turned, second_turned = split_three()
-        scores = matmul(part_of(first, 0), first_turned.astype(BF16), (1, 1)) * SCALE
+        first, turned, value_rows = split_three()
+        scores = matmul(part_of(first, 0), turned.astype(BF16), (1, 1)) * SCALE
         visible = seen(256, 4096 * x + shift_ref[1, own_head], RATE[1])
         scores = jnp.where(visible, scores, HIDDEN)
         scores_three[...] = scores
         top = jnp.max(scores, axis=1, keepdims=True)
         weights = jnp.exp(scores - top)
         total = jnp.sum(weights, axis=1, keepdims=True)
-        out = matmul(weights.astype(BF16), second.astype(BF16), (1, 0)) / total
+        out = matmul(weights.astype(BF16), value_rows, (1, 0)) / total
         lse = jnp.broadcast_to(top + jnp.log(total), (256, 128))
         out = jnp.where(iota((256, 128), 1) < 64, out, lse)
         out_send_three[...] = out.reshape(32, 8, 128)
@@ -418,10 +472,13 @@
             delta_wide[3 * half + tile] = summed[:, 128 * tile : 128 * tile + 128]
 
     picked_lse, picked_delta = pick(lse_wide, 1), pick(delta_wide, 1)
+    picked_grad = pick(source.at[3], 1)
+    lanes = iota((8, 128), 1)
     for head in range(HEADS):
         near = take_window(picked_lse, head * DIM, DIM, 0)
-        far = take_window(picked_delta, head * DIM, DIM, 64)
-        stat_send_three[head] = jnp.where(iota((8, 128), 1) < 64, near, far)
+        middle = take_window(picked_delta, head * DIM, DIM, 32)
+        far = take_window(picked_grad, head * DIM, DIM, 64)
+        stat_send_three[head] = jnp.where(lanes < 32, near, jnp.where(lanes < 64, middle, far))
     picked_lse, picked_delta = pick(lse_wide, 0), pick(delta_wide, 0)
     coded = []
     for tile in range(TILES):
@@ -457,9 +514,10 @@
 
     attended = jnp.concatenate([att_halves[0], att_halves[1]], axis=1)
     mixed_ref[...] = matmul(attended, weight_ref[...], (1, 1)).astype(BF16)
+    outgoing[0].start()
 
     sums_q, sums_k, sums_v = ([None] * TILES for _ in range(3))
-    for head in range(HEADS):
+    def one_back(head):
         lanes, first, span = window(head)
         place = slice(first, first + 1) if first < 128 else slice(first - 128, first - 127)
         lse = lse_wide[span[0]][:, place]
@@ -473,62 +531,9 @@
         merge(sums_q, head, matmul(dscore, k_ref[:, lanes], (1, 0)), True)
         merge(sums_k, head, matmul(dscore, q_ref[:, lanes], (0, 0)), True)
         merge(sums_v, head, matmul(prob.astype(BF16), grad_low, (0, 0)), True)
-    for tile in range(TILES):
-        totals[0, tile] = sums_q[tile]
-        totals[1, tile] = sums_k[tile]
-        totals[2, tile] = sums_v[tile]
-
-    @pl.when(has_head)
-    def _():
-        arrived(stat_recv_three, 7)
-        first, second, first_turned, second_turned = split_three()
-        stats = stat_recv_three[...].reshape(256, 128)
-        prob = jnp.exp(scores_three[...] - stats[:, 0:1])
-        dprob = matmul(part_of(second_turned, 0), second.astype(BF16), (1, 1))
-        dscore = (prob * (dprob - stats[:, 64:65]) * SCALE).astype(BF16)
-        grad_qk = matmul(dscore, part_of(first_turned, 0), (1, 0))
-        grad_qk = grad_qk + matmul(dscore, part_of(first_turned, 64), (0, 0))
-        grad_v = matmul(prob.astype(BF16), part_of(second_turned, 0), (0, 0))
-        grads = jnp.concatenate([grad_qk.reshape(32, 8, 128), grad_v.reshape(32, 8, 128)], axis=1)
-        grad_send_three[...] = grads.astype(BF16)
-
-        @pl.loop(1, 32)
-        def _(step):
-            other = (mine_three + step) % 32
-            push(grad_send_three.at[other], grad_recv_three.at[own_head], 8, plane + other)
-
-        keep(grad_send_three.at[mine_three], grad_recv_three.at[own_head], 8)
-
-    arrived(stat_recv_two, 6)
-    row = iota((128, 256), 0)
-    stats = stat_recv_two[...]
-    grads = [None] * 3
-    for member in range(2):
-
-        def gathered(first):
-            hit = (row == first) | (row == first + 8) | (row == first + 16)
-            return matmul(stats, jnp.where(hit, 1.0, 0.0).astype(BF16), (1, 0))
-
-        prob = jnp.exp(scores_two[member] - gathered(DIM * member))
-        dprob = matmul(masked(recv_two[3], DIM * member, DIM), recv_two[2], (1, 1))
-        dscore = (prob * (dprob - gathered(DIM * member + 24)) * SCALE).astype(BF16)
-        news = (
-            matmul(dscore, recv_two[1], (1, 0)),
-            matmul(dscore, recv_two[0], (0, 0)),
-            matmul(prob.astype(BF16), recv_two[3], (0, 0)),
-        )
-        for index, new in enumerate(news):
-            old = grads[index]
-            grads[index] = new if member == 0 else jnp.where(lanes_two < DIM, old, new)
-    for index in range(3):
-        grad_send_two[index] = grads[index].astype(BF16)
-
-    @pl.loop(1, 8)
-    def _(step):
-        other = (mine_two + step) % 8
-        push(grad_send_two.at[:, pl.ds(32 * other, 32)], grad_recv_two.at[mine_two], 9, block + other)
-
-    keep(grad_send_two.at[:, pl.ds(32 * mine_two, 32)], grad_recv_two.at[mine_two], 9)
+
+    for head in range(EARLY):
+        one_back(head)
 
     arrived(cot_all, 2)
     arrived(att_all, 5)
@@ -547,6 +552,87 @@
         push(z_send.at[other], z_recv.at[z], 10, plane + 4 * other + y)
 
     keep(z_send.at[z], z_recv.at[z], 10)
+
+    @pl.when(has_head)
+    def _():
+        arrived(stat_recv_three, 7)
+        first, turned, value_rows = split_three()
+        stats = stat_recv_three[...].reshape(256, 128)
+        grad_rows = part_of(pltpu.roll(stats, 64, 1), 0)
+        prob = jnp.exp(scores_three[...] - stats[:, 0:1])
+        dprob = matmul(grad_rows, value_rows, (1, 1))
+        dscore = (prob * (dprob - stats[:, 32:33]) * SCALE).astype(BF16)
+        grad_qk = matmul(dscore, part_of(turned, 0), (1, 0))
+        grad_qk = grad_qk + matmul(dscore, part_of(turned, 64), (0, 0))
+        grad_v = matmul(prob.astype(BF16), grad_rows, (0, 0))
+        grads = jnp.concatenate([grad_qk.reshape(32, 8, 128), grad_v.reshape(32, 8, 128)], axis=1)
+        grad_send_three[...] = grads.astype(BF16)
+
+        @pl.loop(1, 32)
+        def _(step):
+            other = (mine_three + step) % 32
+            push(grad_send_three.at[other], grad_recv_three.at[own_head], 8, plane + other)
+
+        keep(grad_send_three.at[mine_three], grad_recv_three.at[own_head], 8)
+
+    arrived(d_recv_two, 12)
+    arrived(stat_recv_two, 6)
+    row = iota((128, 256), 0)
+    stats = stat_recv_two[...]
+    grads = [None] * 3
+    for member in range(2):
+
+        def gathered(first):
+            hit = (row == first) | (row == first + 8) | (row == first + 16)
+            return matmul(stats, jnp.where(hit, 1.0, 0.0).astype(BF16), (1, 0))
+
+        prob = jnp.exp(scores_two[member] - gathered(DIM * member))
+        dprob = matmul(masked(d_recv_two[...], DIM * member, DIM), recv_two[2], (1, 1))
+        dscore = (prob * (dprob - gathered(DIM * member + 24)) * SCALE).astype(BF16)
+        news = (
+            matmul(dscore, recv_two[1], (1, 0)),
+            matmul(dscore, recv_two[0], (0, 0)),
+            matmul(prob.astype(BF16), d_recv_two[...], (0, 0)),
+        )
+        for index, new in enumerate(news):
+            old = grads[index]
+            grads[index] = new if member == 0 else jnp.where(lanes_two < DIM, old, new)
+    for index in range(3):
+        grad_send_two[index] = grads[index].astype(BF16)
+
+    @pl.loop(1, 8)
+    def _(step):
+        other = (mine_two + step) % 8
+        push(grad_send_two.at[:, pl.ds(32 * other, 32)], grad_recv_two.at[mine_two], 9, block + other)
+
+    keep(grad_send_two.at[:, pl.ds(32 * mine_two, 32)], grad_recv_two.at[mine_two], 9)
+
+    for head in range(EARLY, HEADS):
+        one_back(head)
+    for tile in range(TILES):
+        totals[0, tile] = sums_q[tile]
+        totals[1, tile] = sums_k[tile]
+        totals[2, tile] = sums_v[tile]
+
+    arrived(z_recv, 10)
+    rows = z_recv[0].astype(F32)
+    for other in range(1, 8):
+        rows = rows + z_recv[other].astype(F32)
+    part[0:48] = rows
+    for low in range(2):
+        for other in range(4):
+            start = 24 * low + 6 * other
+            y_send[low, other, 0:6] = part[start : start + 6]
+            y_send[low, other, 6:8] = jnp.zeros((2, HALF), F32)
+
+    @pl.loop(1, 8)
+    def _(step):
+        other = (4 * x_low + y + step) % 8
+        low, high = other // 4, other % 4
+        device = (2 * x_high + low) * 32 + 4 * z + high
+        push(y_send.at[low, high], y_recv.at[x_low, y], 11, device)
+
+    keep(y_send.at[x_low, y], y_recv.at[x_low, y], 11)
 
     arrived(grad_recv_three, 8)
     received = grad_recv_three[...].astype(F32)
@@ -559,30 +645,13 @@
         spread(totals.at[index], 0, put_windows(windows, 96, 0), True)
         for tile in range(TILES):
             out_ref[:, 128 * tile : 128 * tile + 128] = totals[index, tile].astype(BF16)
-
-    arrived(z_recv, 10)
-    rows = z_recv[0].astype(F32)
-    for other in range(1, 8):
-        rows = rows + z_recv[other].astype(F32)
-    part[0:48] = rows
-    for low in range(2):
-        for other in range(4):
-            start = 24 * low + 6 * other
-            y_send[low, other, 0:6] = part[start : start + 6]
-            y_send[low, other, 6:8] = jnp.zeros((2, HALF), F32)
-
-    @pl.loop(1, 8)
-    def _(step):
-        other = (4 * x_low + y + step) % 8
-        low, high = other // 4, other % 4
-        device = (2 * x_high + low) * 32 + 4 * z + high
-        push(y_send.at[low, high], y_recv.at[x_low, y], 11, device)
-
-    keep(y_send.at[x_low, y], y_recv.at[x_low, y], 11)
+        outgoing[1 + index].start()
+
     arrived(y_recv, 11)
     for low in range(2):
         rows = (y_recv[low, 0] + y_recv[low, 1]) + (y_recv[low, 2] + y_recv[low, 3])
         dw_ref[:, HALF * low : HALF * low + HALF] = rows[0:6] * (16384**-0.5)
+    outgoing[4].start()
 
     left(send_two.at[0:7], 0)
     left(cot_all.at[0:3], 2)
@@ -591,6 +660,7 @@
     left(stat_send_two.at[0:7], 6)
     left(grad_recv_two.at[0:7], 9)
     left(z_send.at[0:7], 10)
+    left(d_send_two.at[0:7], 12)
     left(y_send.at[0:1], 11)
     left(y_send.at[0, 0:3], 11)
 
@@ -606,15 +676,33 @@
         left(send_three, 1)
         left(stat_send_three, 7)
 
+    for copy in outgoing:
+        copy.wait()
+
+
+def finish(*refs):
+    sources, results, holders, sems = refs[:5], refs[5:10], refs[10:15], refs[15]
+    inward, outward = [], []
+    for index in range(5):
+        inward.append(pltpu.make_async_copy(sources[index], holders[index], sems.at[0, index]))
+        outward.append(pltpu.make_async_copy(holders[index], results[index], sems.at[1, index]))
+        inward[index].start()
+    for index in range(5):
+        inward[index].wait()
+        outward[index].start()
+    for index in range(5):
+        outward[index].wait()
+
 
 def local(queries, keys, values, cotangent, out_weight, slide_lengths, head_dilation_shifts):
-    vmem = pl.BlockSpec(memory_space=pltpu.VMEM)
-    smem = pl.BlockSpec(memory_space=pltpu.SMEM)
+    far = pl.BlockSpec(memory_space=pltpu.HBM)
     wide = jax.ShapeDtypeStruct((ROWS, WIDTH), BF16)
     scratch = [
         ((4, TILES, ROWS, 128), F32),
-        ((8, 4, 32, 128), BF16),
-        ((4, 256, 128), BF16),
+        ((8, 3, 32, 128), BF16),
+        ((3, 256, 128), BF16),
+        ((8, 32, 128), BF16),
+        ((256, 128), BF16),
         ((16, 16, 128), BF16),
         ((32, 16, 128), BF16),
         ((256, 128), BF16),
@@ -647,18 +735,33 @@
         ((TILES, ROWS, 128), F32),
         ((3, TILES, ROWS, 128), F32),
     ]
-    return pl.pallas_call(
+    out_shape = (wide, wide, wide, wide, jax.ShapeDtypeStruct((WIDTH // 128, WIDTH), F32))
+    results = pl.pallas_call(
         kernel,
-        out_shape=(wide, wide, wide, wide, jax.ShapeDtypeStruct((WIDTH // 128, WIDTH), F32)),
-        in_specs=[vmem] * 5 + [smem] * 2,
-        out_specs=(vmem,) * 5,
-        scratch_shapes=[pltpu.VMEM(shape, dtype) for shape, dtype in scratch]
-        + [pltpu.SemaphoreType.DMA((12,)), pltpu.SemaphoreType.DMA((12,))],
+        out_shape=out_shape,
+        in_specs=[far] * 7,
+        out_specs=(far,) * 5,
+        scratch_shapes=[pltpu.VMEM((ROWS, WIDTH), BF16)] * 4
+        + [pltpu.VMEM((WIDTH // 128, WIDTH), F32)]
+        + [pltpu.VMEM((ROWS, WIDTH), BF16)] * 4
+        + [pltpu.VMEM((WIDTH, WIDTH), BF16), pltpu.SMEM((8,), jnp.int32), pltpu.SMEM((2, HEADS), jnp.int32)]
+        + [pltpu.VMEM(shape, dtype) for shape, dtype in scratch]
+        + [pltpu.SemaphoreType.DMA((13,)), pltpu.SemaphoreType.DMA((13,)), pltpu.SemaphoreType.DMA((7,)), pltpu.SemaphoreType.DMA((5,))],
         compiler_params=pltpu.CompilerParams(
-            collective_id=0, has_side_effects=True, vmem_limit_bytes=48 * 1024 * 1024
+            collective_id=0, has_side_effects=True, vmem_limit_bytes=VMEM
         ),
         name="dilated_attention",
     )(queries, keys, values, cotangent, out_weight, slide_lengths, head_dilation_shifts)
+    return pl.pallas_call(
+        finish,
+        out_shape=out_shape,
+        in_specs=[far] * 5,
+        out_specs=(far,) * 5,
+        scratch_shapes=[pltpu.VMEM(shape.shape, shape.dtype) for shape in out_shape]
+        + [pltpu.SemaphoreType.DMA((2, 5))],
+        compiler_params=pltpu.CompilerParams(vmem_limit_bytes=VMEM),
+        name="results_to_hbm",
+    )(*results)
 
 
 def solution(mesh):

time: 66.2 us -> 51.7 us (0.78)
  local copies, waits for them, and re-layouts: 9.62 us -> 0 us
  Pallas kernels: 55.6 us -> 50.8 us
    unnamed x19 -> x0, local copies, waits for them, and re-layouts: 9.62 us -> none
    pallas_call x1 -> x2, Pallas kernels: 55.6 us -> 50.8 us  [the longest x1 48.9 us: local(): pl.pallas_call(kernel, out_shape=out_shape, in_specs=[far] * 7, out_specs...]
where the time goes in v2:
time: 51.7 us; the launch traced here: 51.5 us
  Pallas kernels  50.8 us (98%)
  between operations  0.64 us (1%)
    pallas_call x1, Pallas kernels, local(): pl.pallas_call(kernel, out_shape=out_shape, in_specs=[far] * 7, out_specs...  48.9 us
    pallas_call x1, Pallas kernels, local(): pl.pallas_call(finish, out_shape=out_shape, in_specs=[far] * 5, out_specs...  1.99 us

profile of v2, /device:TPU:56, one launch (start us, length us, event | category | flops | bytes accessed | tf_op | source)
XLA Modules:
  0.0 51.5 jit_solution(12211853508143554321)
XLA Ops:
  0.6 48.9 %dilated_attention.1 = (bf16[128,768]{1,0:T(8,128)(2,1)}, bf16[128,768]{1,0:T(8,128)(2,1)}, bf16[128,768]{1,0:T(8,128)(2,1)}, bf16[128,768]{1,0:T(8,128)(2,1)}, f32[6,768]{1,0:T(8,128)}) custom-call(bf16[128,768]{1,0:T(8,128)(2,1)} %q_far.1, bf16[128,768]{1,0:T(8,128)(2,1)} %k_far.1, bf16[128,768]{1,0:T(8,128)(2,1)} %v_far.1, bf16[128,768]{1,0:T(8,128)(2,1)} %cot_far.1, ...), custom_call_target="tpu_custom_call" | custom-call | tf_op jit(solution)/shard_map/dilated_attention/pallas_call | solution.py:739
  49.5 2.0 %results_to_hbm.1 = (bf16[128,768]{1,0:T(8,128)(2,1)}, bf16[128,768]{1,0:T(8,128)(2,1)}, bf16[128,768]{1,0:T(8,128)(2,1)}, bf16[128,768]{1,0:T(8,128)(2,1)}, f32[6,768]{1,0:T(8,128)}) custom-call(bf16[128,768]{1,0:T(8,128)(2,1)} %get-tuple-element.10.refs_0_, bf16[128,768]{1,0:T(8,128)(2,1)} %get-tuple-element.11.refs_1_, ...), custom_call_target="tpu_custom_call" | custom-call | tf_op jit(solution)/shard_map/results_to_hbm/pallas_call | solution.py:755

commit v3 on v2

--- a/solution.py
+++ b/solution.py
@@ -15,7 +15,7 @@
 COUNT = (ROWS // 4, ROWS // 16)
 SCALE = DIM**-0.5
 HIDDEN = -1e30
-EARLY = 8
+EARLY = (0, 2, 4, 6)
 VMEM = 60 * 1024 * 1024
 F32 = jnp.float32
 BF16 = jnp.bfloat16
@@ -121,6 +121,7 @@
     cot_all,
     att_all,
     part,
+    block_rows,
     z_send,
     z_recv,
     y_send,
@@ -138,6 +139,39 @@
     in_sems,
     out_sems,
 ):
+    rank = lax.axis_index("seq")
+    x, z, y = rank // 32, (rank % 32) // 4, rank % 4
+    x_high, x_low = x // 2, x % 2
+    plane, mine_three = rank - rank % 32, rank % 32
+    block, mine_two = rank - rank % 8, rank % 8
+    has_head = (y == 1) | (y == 2)
+    own_head = 2 * z + jnp.where(y == 2, 1, 0)
+
+    def worker(head):
+        return 4 * (head // 2) + 1 + head % 2
+
+    def outward(step, count):
+        return count // 2 + (1 - 2 * (step % 2)) * ((step + 1) // 2)
+
+    barrier = pltpu.get_barrier_semaphore()
+
+    def greet(device):
+        pl.semaphore_signal(barrier, inc=1, device_id={"seq": device}, device_id_type=MESH)
+
+    @pl.loop(0, 31)
+    def _(step):
+        greet(plane + (mine_three + outward(step, 32)) % 32)
+
+    @pl.loop(1, 4)
+    def _(step):
+        greet(((x + step) % 4) * 32 + mine_three)
+
+    other_x = 2 * x_high + 1 - x_low
+
+    @pl.loop(1, 4)
+    def _(step):
+        greet(other_x * 32 + z * 4 + (y + step) % 4)
+
     pairs = (
         (shift_far, shift_ref),
         (q_far, q_ref),
@@ -159,36 +193,6 @@
     )
     outgoing = [pltpu.make_async_copy(*pair, out_sems.at[index]) for index, pair in enumerate(pairs)]
 
-    rank = lax.axis_index("seq")
-    x, z, y = rank // 32, (rank % 32) // 4, rank % 4
-    x_high, x_low = x // 2, x % 2
-    plane, mine_three = rank - rank % 32, rank % 32
-    block, mine_two = rank - rank % 8, rank % 8
-    has_head = mine_three % 2 == (mine_three // 4) % 2
-    own_head = mine_three // 2
-
-    def worker(head):
-        return 2 * head + (head // 2) % 2
-
-    barrier = pltpu.get_barrier_semaphore()
-
-    def greet(device):
-        pl.semaphore_signal(barrier, inc=1, device_id={"seq": device}, device_id_type=MESH)
-
-    @pl.loop(1, 32)
-    def _(step):
-        greet(plane + (mine_three + step) % 32)
-
-    @pl.loop(1, 4)
-    def _(step):
-        greet(((x + step) % 4) * 32 + mine_three)
-
-    other_x = 2 * x_high + 1 - x_low
-
-    @pl.loop(1, 4)
-    def _(step):
-        greet(other_x * 32 + z * 4 + (y + step) % 4)
-
     def push(from_ref, to_ref, index, device):
         pltpu.make_async_remote_copy(
             src_ref=from_ref,
@@ -256,7 +260,7 @@
 
     @pl.loop(0, HEADS)
     def _(step):
-        head = (own_head + step) % HEADS
+        head = (2 * z + outward(step, HEADS) + HEADS) % HEADS
         other = worker(head)
 
         @pl.when(other != mine_three)
@@ -290,20 +294,6 @@
         push(cot_halves.at[other // 2], cot_all.at[x], 2, other * 32 + mine_three)
 
     keep(cot_halves.at[x_high], cot_all.at[x], 2)
-    d_attended = jnp.dot(cot_ref[...], weight_ref[...], preferred_element_type=F32).astype(BF16)
-    for tile in range(TILES):
-        source[3, tile] = d_attended[:, 128 * tile : 128 * tile + 128].astype(F32)
-    picked = pick(source.at[3], 0)
-    for other in range(8):
-        d_send_two[other] = take_window(picked, 96 * other, 96, 0).astype(BF16)
-
-    @pl.loop(1, 8)
-    def _(step):
-        other = (mine_two + step) % 8
-        push(d_send_two.at[other], d_recv_two.at[pl.ds(32 * mine_two, 32)], 12, block + other)
-
-    keep(d_send_two.at[mine_two], d_recv_two.at[pl.ds(32 * mine_two, 32)], 12)
-
     ends = []
     running = 0
     for index in range(8):
@@ -389,9 +379,9 @@
         out = jnp.where(iota((256, 128), 1) < 64, out, lse)
         out_send_three[...] = out.reshape(32, 8, 128)
 
-        @pl.loop(1, 32)
+        @pl.loop(0, 31)
         def _(step):
-            other = (mine_three + step) % 32
+            other = (mine_three + outward(step, 32)) % 32
             push(out_send_three.at[other], out_recv_three.at[own_head], 3, plane + other)
 
         keep(out_send_three.at[mine_three], out_recv_three.at[own_head], 3)
@@ -423,6 +413,20 @@
         push(out_send_two.at[pl.ds(32 * other, 32)], out_recv_two.at[mine_two], 4, block + other)
 
     keep(out_send_two.at[pl.ds(32 * mine_two, 32)], out_recv_two.at[mine_two], 4)
+
+    d_attended = jnp.dot(cot_ref[...], weight_ref[...], preferred_element_type=F32).astype(BF16)
+    for tile in range(TILES):
+        source[3, tile] = d_attended[:, 128 * tile : 128 * tile + 128].astype(F32)
+    picked = pick(source.at[3], 0)
+    for other in range(8):
+        d_send_two[other] = take_window(picked, 96 * other, 96, 0).astype(BF16)
+
+    @pl.loop(1, 8)
+    def _(step):
+        other = (mine_two + step) % 8
+        push(d_send_two.at[other], d_recv_two.at[pl.ds(32 * mine_two, 32)], 12, block + other)
+
+    keep(d_send_two.at[mine_two], d_recv_two.at[pl.ds(32 * mine_two, 32)], 12)
 
     arrived(out_recv_three, 3)
     out_three = put_windows([out_recv_three[head] for head in range(HEADS)], DIM, 0)
@@ -450,21 +454,22 @@
         for level in range(3):
             share = jnp.exp(levels[level] - lse)
             combined = combined + jnp.where(share > 0, share * level_out[level, tile], 0.0)
-        half, place = tile // 3, 128 * (tile % 3)
-        att_halves[half, :, place : place + 128] = combined.astype(BF16)
-
-    @pl.loop(1, 4)
-    def _(step):
-        other = (x + step) % 4
-        push(att_halves.at[other % 2], att_all.at[x], 5, other * 32 + mine_three)
-
-    keep(att_halves.at[x_low], att_all.at[x], 5)
+        att_halves[tile // 3, tile % 3] = combined.astype(BF16)
+
+    for chunk in range(3):
+
+        for step in (2, 1, 3):
+            other = (x + step) % 4
+            device = other * 32 + mine_three
+            push(att_halves.at[other % 2, chunk], att_all.at[chunk, x], 13 + chunk, device)
+
+        keep(att_halves.at[x_low, chunk], att_all.at[chunk, x], 13 + chunk)
 
     same_head = over_48(iota((HALF, HALF), 0)) == over_48(iota((HALF, HALF), 1))
     same_head = jnp.where(same_head, 1.0, 0.0).astype(BF16)
     for half in range(2):
         product = jnp.concatenate([source[3, 3 * half + tile] for tile in range(3)], axis=1)
-        product = product * att_halves[half].astype(F32)
+        product = product * jnp.concatenate([att_halves[half, tile].astype(F32) for tile in range(3)], axis=1)
         high, middle, low = three_parts(product)
         summed = matmul(high.astype(BF16), same_head, (1, 0))
         summed = summed + matmul(middle.astype(BF16), same_head, (1, 0))
@@ -501,7 +506,7 @@
 
     @pl.loop(0, HEADS)
     def _(step):
-        head = (own_head + step) % HEADS
+        head = (2 * z + outward(step, HEADS) + HEADS) % HEADS
         other = worker(head)
 
         @pl.when(other != mine_three)
@@ -512,7 +517,7 @@
     def _():
         keep(stat_send_three.at[own_head], stat_recv_three.at[mine_three], 7)
 
-    attended = jnp.concatenate([att_halves[0], att_halves[1]], axis=1)
+    attended = jnp.concatenate([att_halves[tile // 3, tile % 3] for tile in range(TILES)], axis=1)
     mixed_ref[...] = matmul(attended, weight_ref[...], (1, 1)).astype(BF16)
     outgoing[0].start()
 
@@ -532,26 +537,25 @@
         merge(sums_k, head, matmul(dscore, q_ref[:, lanes], (0, 0)), True)
         merge(sums_v, head, matmul(prob.astype(BF16), grad_low, (0, 0)), True)
 
-    for head in range(EARLY):
-        one_back(head)
-
     arrived(cot_all, 2)
-    arrived(att_all, 5)
-    part[...] = matmul(
-        cot_all[...].reshape(4 * ROWS, HALF), att_all[...].reshape(4 * ROWS, HALF), (0, 0)
-    )
-    for other in range(8):
-        rows = jnp.concatenate(
-            [part[24 * other : 24 * other + 24], part[192 + 24 * other : 216 + 24 * other]], axis=0
+    for chunk in range(3):
+        for head in range(EARLY[chunk], EARLY[chunk + 1]):
+            one_back(head)
+        arrived(att_all.at[chunk], 13 + chunk)
+        part[chunk] = matmul(
+            cot_all[...].reshape(4 * ROWS, HALF), att_all[chunk].reshape(4 * ROWS, 128), (0, 0)
         )
-        z_send[other] = rows.astype(BF16)
-
-    @pl.loop(1, 8)
-    def _(step):
-        other = (z + step) % 8
-        push(z_send.at[other], z_recv.at[z], 10, plane + 4 * other + y)
-
-    keep(z_send.at[z], z_recv.at[z], 10)
+        for other in range(8):
+            near = part[chunk, 24 * other : 24 * other + 24]
+            far = part[chunk, 192 + 24 * other : 216 + 24 * other]
+            z_send[chunk, other] = jnp.concatenate([near, far], axis=0).astype(BF16)
+
+        for step in (4, 3, 5, 2, 6, 1, 7):
+            other = (z + step) % 8
+            device = plane + 4 * other + y
+            push(z_send.at[chunk, other], z_recv.at[chunk, z], 16 + chunk, device)
+
+        keep(z_send.at[chunk, z], z_recv.at[chunk, z], 16 + chunk)
 
     @pl.when(has_head)
     def _():
@@ -568,9 +572,9 @@
         grads = jnp.concatenate([grad_qk.reshape(32, 8, 128), grad_v.reshape(32, 8, 128)], axis=1)
         grad_send_three[...] = grads.astype(BF16)
 
-        @pl.loop(1, 32)
+        @pl.loop(0, 31)
         def _(step):
-            other = (mine_three + step) % 32
+            other = (mine_three + outward(step, 32)) % 32
             push(grad_send_three.at[other], grad_recv_three.at[own_head], 8, plane + other)
 
         keep(grad_send_three.at[mine_three], grad_recv_three.at[own_head], 8)
@@ -607,32 +611,33 @@
 
     keep(grad_send_two.at[:, pl.ds(32 * mine_two, 32)], grad_recv_two.at[mine_two], 9)
 
-    for head in range(EARLY, HEADS):
+    for chunk in range(3):
+        arrived(z_recv.at[chunk], 16 + chunk)
+        rows = z_recv[chunk, 0].astype(F32)
+        for other in range(1, 8):
+            rows = rows + z_recv[chunk, other].astype(F32)
+        block_rows[:, 128 * chunk : 128 * chunk + 128] = rows
+    for low in range(2):
+        for other in range(4):
+            start = 24 * low + 6 * other
+            y_send[low, other, 0:6] = block_rows[start : start + 6]
+            y_send[low, other, 6:8] = jnp.zeros((2, HALF), F32)
+
+    @pl.loop(1, 8)
+    def _(step):
+        other = (4 * x_low + y + step) % 8
+        low, high = other // 4, other % 4
+        device = (2 * x_high + low) * 32 + 4 * z + high
+        push(y_send.at[low, high], y_recv.at[x_low, y], 11, device)
+
+    keep(y_send.at[x_low, y], y_recv.at[x_low, y], 11)
+
+    for head in range(EARLY[3], HEADS):
         one_back(head)
     for tile in range(TILES):
         totals[0, tile] = sums_q[tile]
         totals[1, tile] = sums_k[tile]
         totals[2, tile] = sums_v[tile]
-
-    arrived(z_recv, 10)
-    rows = z_recv[0].astype(F32)
-    for other in range(1, 8):
-        rows = rows + z_recv[other].astype(F32)
-    part[0:48] = rows
-    for low in range(2):
-        for other in range(4):
-            start = 24 * low + 6 * other
-            y_send[low, other, 0:6] = part[start : start + 6]
-            y_send[low, other, 6:8] = jnp.zeros((2, HALF), F32)
-
-    @pl.loop(1, 8)
-    def _(step):
-        other = (4 * x_low + y + step) % 8
-        low, high = other // 4, other % 4
-        device = (2 * x_high + low) * 32 + 4 * z + high
-        push(y_send.at[low, high], y_recv.at[x_low, y], 11, device)
-
-    keep(y_send.at[x_low, y], y_recv.at[x_low, y], 11)
 
     arrived(grad_recv_three, 8)
     received = grad_recv_three[...].astype(F32)
@@ -656,10 +661,11 @@
     left(send_two.at[0:7], 0)
     left(cot_all.at[0:3], 2)
     left(out_send_two.at[0:224], 4)
-    left(att_all.at[0:3], 5)
+    for chunk in range(3):
+        left(att_all.at[chunk, 0:3], 13 + chunk)
+        left(z_send.at[chunk, 0:7], 16 + chunk)
     left(stat_send_two.at[0:7], 6)
     left(grad_recv_two.at[0:7], 9)
-    left(z_send.at[0:7], 10)
     left(d_send_two.at[0:7], 12)
     left(y_send.at[0:1], 11)
     left(y_send.at[0, 0:3], 11)
@@ -718,12 +724,13 @@
         ((32, 16, 128), BF16),
         ((16, 16, 128), BF16),
         ((2, ROWS, HALF), BF16),
-        ((2, ROWS, HALF), BF16),
+        ((2, 3, ROWS, 128), BF16),
         ((4, ROWS, HALF), BF16),
-        ((4, ROWS, HALF), BF16),
-        ((HALF, HALF), F32),
-        ((8, 48, HALF), BF16),
-        ((8, 48, HALF), BF16),
+        ((3, 4, ROWS, 128), BF16),
+        ((3, HALF, 128), F32),
+        ((48, HALF), F32),
+        ((3, 8, 48, 128), BF16),
+        ((3, 8, 48, 128), BF16),
         ((2, 4, 8, HALF), F32),
         ((2, 4, 8, HALF), F32),
         ((HEADS, ROWS, ROWS), F32),
@@ -746,7 +753,7 @@
         + [pltpu.VMEM((ROWS, WIDTH), BF16)] * 4
         + [pltpu.VMEM((WIDTH, WIDTH), BF16), pltpu.SMEM((8,), jnp.int32), pltpu.SMEM((2, HEADS), jnp.int32)]
         + [pltpu.VMEM(shape, dtype) for shape, dtype in scratch]
-        + [pltpu.SemaphoreType.DMA((13,)), pltpu.SemaphoreType.DMA((13,)), pltpu.SemaphoreType.DMA((7,)), pltpu.SemaphoreType.DMA((5,))],
+        + [pltpu.SemaphoreType.DMA((19,)), pltpu.SemaphoreType.DMA((19,)), pltpu.SemaphoreType.DMA((7,)), pltpu.SemaphoreType.DMA((5,))],
         compiler_params=pltpu.CompilerParams(
             collective_id=0, has_side_effects=True, vmem_limit_bytes=VMEM
         ),

time: 51.7 us -> 49.8 us (0.963)
  Pallas kernels: 50.8 us -> 49 us
    pallas_call x1, Pallas kernels: 48.9 us -> 47 us  [local(): pl.pallas_call(kernel, out_shape=out_shape, in_specs=[far] * 7, out_specs...]
where the time goes in v3:
time: 49.8 us; the launch traced here: 49.6 us
  Pallas kernels  49 us (98%)
  between operations  0.64 us (1%)
    pallas_call x1, Pallas kernels, local(): pl.pallas_call(kernel, out_shape=out_shape, in_specs=[far] * 7, out_specs...  47 us
    pallas_call x1, Pallas kernels, local(): pl.pallas_call(finish, out_shape=out_shape, in_specs=[far] * 5, out_specs...  1.99 us

profile of v3, /device:TPU:56, one launch (start us, length us, event | category | flops | bytes accessed | tf_op | source)
XLA Modules:
  0.0 49.6 jit_solution(12305485372146980376)
XLA Ops:
  0.6 47.0 %dilated_attention.1 = (bf16[128,768]{1,0:T(8,128)(2,1)}, bf16[128,768]{1,0:T(8,128)(2,1)}, bf16[128,768]{1,0:T(8,128)(2,1)}, bf16[128,768]{1,0:T(8,128)(2,1)}, f32[6,768]{1,0:T(8,128)}) custom-call(bf16[128,768]{1,0:T(8,128)(2,1)} %q_far.1, bf16[128,768]{1,0:T(8,128)(2,1)} %k_far.1, bf16[128,768]{1,0:T(8,128)(2,1)} %v_far.1, bf16[128,768]{1,0:T(8,128)(2,1)} %cot_far.1, ...), custom_call_target="tpu_custom_call" | custom-call | tf_op jit(solution)/shard_map/dilated_attention/pallas_call | solution.py:746
  47.6 2.0 %results_to_hbm.1 = (bf16[128,768]{1,0:T(8,128)(2,1)}, bf16[128,768]{1,0:T(8,128)(2,1)}, bf16[128,768]{1,0:T(8,128)(2,1)}, bf16[128,768]{1,0:T(8,128)(2,1)}, f32[6,768]{1,0:T(8,128)}) custom-call(bf16[128,768]{1,0:T(8,128)(2,1)} %get-tuple-element.10.refs_0_, bf16[128,768]{1,0:T(8,128)(2,1)} %get-tuple-element.11.refs_1_, ...), custom_call_target="tpu_custom_call" | custom-call | tf_op jit(solution)/shard_map/results_to_hbm/pallas_call | solution.py:762

commit v4 on v3

--- a/solution.py
+++ b/solution.py
@@ -15,7 +15,7 @@
 COUNT = (ROWS // 4, ROWS // 16)
 SCALE = DIM**-0.5
 HIDDEN = -1e30
-EARLY = (0, 2, 4, 6)
+EARLY = (0, 3, 5, 7)
 VMEM = 60 * 1024 * 1024
 F32 = jnp.float32
 BF16 = jnp.bfloat16
@@ -124,6 +124,13 @@
     block_rows,
     z_send,
     z_recv,
+    same_head_ref,
+    widen_ref,
+    last_rows,
+    last_send,
+    last_recv,
+    w_send,
+    w_recv,
     y_send,
     y_recv,
     scores_one,
@@ -172,6 +179,10 @@
     def _(step):
         greet(other_x * 32 + z * 4 + (y + step) % 4)
 
+    @pl.loop(1, 8)
+    def _(step):
+        greet(other_x * 32 + (z + step) % 8 * 4 + y)
+
     pairs = (
         (shift_far, shift_ref),
         (q_far, q_ref),
@@ -239,11 +250,11 @@
             tiles.append(value)
         return tiles
 
-    def spread(view, level, tiles, add):
+    def spread(view, level, tiles, add, fill=0.0):
         for tile in range(TILES):
             for offset in range(RATE[level]):
                 place = (tile, pl.ds(offset, COUNT[level], RATE[level]), slice(None))
-                other = view[place] if add else HIDDEN
+                other = view[place] if add else fill
                 value = tiles[tile] + other if add else tiles[tile]
                 view[place] = jnp.where(shifts[level][tile] == offset, value, other)
 
@@ -256,7 +267,7 @@
         totals[0, 0, 8:16] = take_window(picked_three[2], head * DIM, DIM, 0)
         send_three[head] = totals[0, 0, 0:16].astype(BF16)
 
-    pl.semaphore_wait(barrier, 37)
+    pl.semaphore_wait(barrier, 44)
 
     @pl.loop(0, HEADS)
     def _(step):
@@ -323,6 +334,14 @@
     def window(head):
         span = tile_span(head * DIM, DIM)
         return slice(128 * span[0], 128 * (span[-1] + 1)), head * DIM - 128 * span[0], span
+
+    same_head = over_48(iota((HALF, HALF), 0)) == over_48(iota((HALF, HALF), 1))
+    same_head_ref[...] = jnp.where(same_head, 1.0, 0.0).astype(BF16)
+    row, column = iota((128, 128), 0), iota((128, 128), 1)
+    widen = ((row >= 96) & (row < 99) & (column < DIM)) | (
+        (row >= 112) & (row < 115) & (column >= DIM) & (column < 96)
+    )
+    widen_ref[...] = jnp.where(widen, 1.0, 0.0).astype(BF16)
 
     visible_one = seen(ROWS, ROWS * rank, 1)
     outs, tops, sums = ([None] * TILES for _ in range(3))
@@ -432,41 +451,32 @@
     out_three = put_windows([out_recv_three[head] for head in range(HEADS)], DIM, 0)
     lse_three = put_windows([out_recv_three[head] for head in range(HEADS)], DIM, 64)
     spread(level_out.at[2], 1, out_three, False)
-    spread(level_lse.at[2], 1, lse_three, False)
+    spread(level_lse.at[2], 1, lse_three, False, HIDDEN)
     arrived(out_recv_two, 4)
-    row, column = iota((128, 128), 0), iota((128, 128), 1)
-    widen = ((row >= 96) & (row < 99) & (column < DIM)) | (
-        (row >= 112) & (row < 115) & (column >= DIM) & (column < 96)
-    )
-    widen = jnp.where(widen, 1.0, 0.0).astype(BF16)
     all_two = out_recv_two[...].reshape(256, 128)
-    lse_all = matmul(all_two, widen, (1, 0)).reshape(8, 32, 128)
+    lse_all = matmul(all_two, widen_ref[...], (1, 0)).reshape(8, 32, 128)
     out_all = all_two.astype(F32).reshape(8, 32, 128)
     spread(level_out.at[1], 0, put_windows([out_all[i] for i in range(8)], 96, 0), False)
-    spread(level_lse.at[1], 0, put_windows([lse_all[i] for i in range(8)], 96, 0), False)
-    for tile in range(TILES):
-        levels = [level_lse[level, tile] for level in range(3)]
-        best = jnp.maximum(jnp.maximum(levels[0], levels[1]), levels[2])
-        mass = sum(jnp.exp(level - best) for level in levels)
-        lse = best + jnp.log(mass)
-        lse_wide[tile] = lse
-        combined = jnp.zeros((ROWS, 128), F32)
-        for level in range(3):
-            share = jnp.exp(levels[level] - lse)
-            combined = combined + jnp.where(share > 0, share * level_out[level, tile], 0.0)
-        att_halves[tile // 3, tile % 3] = combined.astype(BF16)
-
+    spread(level_lse.at[1], 0, put_windows([lse_all[i] for i in range(8)], 96, 0), False, HIDDEN)
     for chunk in range(3):
-
+        for half in range(2):
+            tile = 3 * half + chunk
+            levels = [level_lse[level, tile] for level in range(3)]
+            best = jnp.maximum(jnp.maximum(levels[0], levels[1]), levels[2])
+            shares = [jnp.exp(level - best) for level in levels]
+            mass = shares[0] + shares[1] + shares[2]
+            combined = shares[0] * level_out[0, tile]
+            for level in range(1, 3):
+                combined = combined + shares[level] * level_out[level, tile]
+            att_halves[half, chunk] = (combined / mass).astype(BF16)
+            lse_wide[tile] = best + jnp.log(mass)
         for step in (2, 1, 3):
             other = (x + step) % 4
             device = other * 32 + mine_three
             push(att_halves.at[other % 2, chunk], att_all.at[chunk, x], 13 + chunk, device)
-
         keep(att_halves.at[x_low, chunk], att_all.at[chunk, x], 13 + chunk)
 
-    same_head = over_48(iota((HALF, HALF), 0)) == over_48(iota((HALF, HALF), 1))
-    same_head = jnp.where(same_head, 1.0, 0.0).astype(BF16)
+    same_head = same_head_ref[...]
     for half in range(2):
         product = jnp.concatenate([source[3, 3 * half + tile] for tile in range(3)], axis=1)
         product = product * jnp.concatenate([att_halves[half, tile].astype(F32) for tile in range(3)], axis=1)
@@ -484,6 +494,19 @@
         middle = take_window(picked_delta, head * DIM, DIM, 32)
         far = take_window(picked_grad, head * DIM, DIM, 64)
         stat_send_three[head] = jnp.where(lanes < 32, near, jnp.where(lanes < 64, middle, far))
+    @pl.loop(0, HEADS)
+    def _(step):
+        head = (2 * z + outward(step, HEADS) + HEADS) % HEADS
+        other = worker(head)
+
+        @pl.when(other != mine_three)
+        def _():
+            push(stat_send_three.at[head], stat_recv_three.at[mine_three], 7, plane + other)
+
+    @pl.when(has_head)
+    def _():
+        keep(stat_send_three.at[own_head], stat_recv_three.at[mine_three], 7)
+
     picked_lse, picked_delta = pick(lse_wide, 0), pick(delta_wide, 0)
     coded = []
     for tile in range(TILES):
@@ -503,23 +526,6 @@
         push(stat_send_two.at[other], stat_recv_two.at[pl.ds(32 * mine_two, 32)], 6, block + other)
 
     keep(stat_send_two.at[mine_two], stat_recv_two.at[pl.ds(32 * mine_two, 32)], 6)
-
-    @pl.loop(0, HEADS)
-    def _(step):
-        head = (2 * z + outward(step, HEADS) + HEADS) % HEADS
-        other = worker(head)
-
-        @pl.when(other != mine_three)
-        def _():
-            push(stat_send_three.at[head], stat_recv_three.at[mine_three], 7, plane + other)
-
-    @pl.when(has_head)
-    def _():
-        keep(stat_send_three.at[own_head], stat_recv_three.at[mine_three], 7)
-
-    attended = jnp.concatenate([att_halves[tile // 3, tile % 3] for tile in range(TILES)], axis=1)
-    mixed_ref[...] = matmul(attended, weight_ref[...], (1, 1)).astype(BF16)
-    outgoing[0].start()
 
     sums_q, sums_k, sums_v = ([None] * TILES for _ in range(3))
     def one_back(head):
@@ -545,17 +551,30 @@
         part[chunk] = matmul(
             cot_all[...].reshape(4 * ROWS, HALF), att_all[chunk].reshape(4 * ROWS, 128), (0, 0)
         )
-        for other in range(8):
-            near = part[chunk, 24 * other : 24 * other + 24]
-            far = part[chunk, 192 + 24 * other : 216 + 24 * other]
-            z_send[chunk, other] = jnp.concatenate([near, far], axis=0).astype(BF16)
-
-        for step in (4, 3, 5, 2, 6, 1, 7):
-            other = (z + step) % 8
-            device = plane + 4 * other + y
-            push(z_send.at[chunk, other], z_recv.at[chunk, z], 16 + chunk, device)
-
-        keep(z_send.at[chunk, z], z_recv.at[chunk, z], 16 + chunk)
+        if chunk < 2:
+            for other in range(8):
+                near = part[chunk, 24 * other : 24 * other + 24]
+                far = part[chunk, 192 + 24 * other : 216 + 24 * other]
+                z_send[chunk, other] = jnp.concatenate([near, far], axis=0).astype(BF16)
+            for step in (4, 3, 5, 2, 6, 1, 7):
+                other = (z + step) % 8
+                device = plane + 4 * other + y
+                push(z_send.at[chunk, other], z_recv.at[chunk, z], 16 + chunk, device)
+            keep(z_send.at[chunk, z], z_recv.at[chunk, z], 16 + chunk)
+
+    for other in range(4):
+        for group in range(16):
+            start = 24 * group + 6 * other
+            last_rows[8 * group : 8 * group + 6] = part[2, start : start + 6]
+            last_rows[8 * group + 6 : 8 * group + 8] = jnp.zeros((2, 128), F32)
+        last_send[other] = last_rows[...].astype(BF16)
+
+    @pl.loop(1, 4)
+    def _(step):
+        other = (y + step) % 4
+        push(last_send.at[other], last_recv.at[y], 18, plane + 4 * z + other)
+
+    keep(last_send.at[y], last_recv.at[y], 18)
 
     @pl.when(has_head)
     def _():
@@ -611,7 +630,21 @@
 
     keep(grad_send_two.at[:, pl.ds(32 * mine_two, 32)], grad_recv_two.at[mine_two], 9)
 
-    for chunk in range(3):
+    arrived(last_recv, 18)
+    rows = (last_recv[0].astype(F32) + last_recv[1].astype(F32)) + (
+        last_recv[2].astype(F32) + last_recv[3].astype(F32)
+    )
+    w_send[...] = rows.reshape(16, 8, 128)
+
+    @pl.loop(0, 15)
+    def _(step):
+        other = (8 * x_low + z + outward(step, 16)) % 16
+        low, high = other // 8, other % 8
+        device = (2 * x_high + low) * 32 + 4 * high + y
+        push(w_send.at[other], w_recv.at[8 * x_low + z], 10, device)
+
+    keep(w_send.at[8 * x_low + z], w_recv.at[8 * x_low + z], 10)
+    for chunk in range(2):
         arrived(z_recv.at[chunk], 16 + chunk)
         rows = z_recv[chunk, 0].astype(F32)
         for other in range(1, 8):
@@ -621,7 +654,7 @@
         for other in range(4):
             start = 24 * low + 6 * other
             y_send[low, other, 0:6] = block_rows[start : start + 6]
-            y_send[low, other, 6:8] = jnp.zeros((2, HALF), F32)
+            y_send[low, other, 6:8] = jnp.zeros((2, 256), F32)
 
     @pl.loop(1, 8)
     def _(step):
@@ -632,6 +665,9 @@
 
     keep(y_send.at[x_low, y], y_recv.at[x_low, y], 11)
 
+    attended = jnp.concatenate([att_halves[tile // 3, tile % 3] for tile in range(TILES)], axis=1)
+    mixed_ref[...] = matmul(attended, weight_ref[...], (1, 1)).astype(BF16)
+    outgoing[0].start()
     for head in range(EARLY[3], HEADS):
         one_back(head)
     for tile in range(TILES):
@@ -655,7 +691,13 @@
     arrived(y_recv, 11)
     for low in range(2):
         rows = (y_recv[low, 0] + y_recv[low, 1]) + (y_recv[low, 2] + y_recv[low, 3])
-        dw_ref[:, HALF * low : HALF * low + HALF] = rows[0:6] * (16384**-0.5)
+        dw_ref[:, HALF * low : HALF * low + 256] = rows[0:6] * (16384**-0.5)
+    arrived(w_recv, 10)
+    for low in range(2):
+        rows = w_recv[8 * low]
+        for other in range(1, 8):
+            rows = rows + w_recv[8 * low + other]
+        dw_ref[:, HALF * low + 256 : HALF * low + HALF] = rows[0:6] * (16384**-0.5)
     outgoing[4].start()
 
     left(send_two.at[0:7], 0)
@@ -663,10 +705,13 @@
     left(out_send_two.at[0:224], 4)
     for chunk in range(3):
         left(att_all.at[chunk, 0:3], 13 + chunk)
-        left(z_send.at[chunk, 0:7], 16 + chunk)
     left(stat_send_two.at[0:7], 6)
     left(grad_recv_two.at[0:7], 9)
     left(d_send_two.at[0:7], 12)
+    left(z_send.at[0, 0:7], 16)
+    left(z_send.at[1, 0:7], 17)
+    left(last_send.at[0:3], 18)
+    left(w_send.at[0:15], 10)
     left(y_send.at[0:1], 11)
     left(y_send.at[0, 0:3], 11)
 
@@ -728,11 +773,18 @@
         ((4, ROWS, HALF), BF16),
         ((3, 4, ROWS, 128), BF16),
         ((3, HALF, 128), F32),
-        ((48, HALF), F32),
-        ((3, 8, 48, 128), BF16),
-        ((3, 8, 48, 128), BF16),
-        ((2, 4, 8, HALF), F32),
-        ((2, 4, 8, HALF), F32),
+        ((48, 256), F32),
+        ((2, 8, 48, 128), BF16),
+        ((2, 8, 48, 128), BF16),
+        ((HALF, HALF), BF16),
+        ((128, 128), BF16),
+        ((128, 128), F32),
+        ((4, 128, 128), BF16),
+        ((4, 128, 128), BF16),
+        ((16, 8, 128), F32),
+        ((16, 8, 128), F32),
+        ((2, 4, 8, 256), F32),
+        ((2, 4, 8, 256), F32),
         ((HEADS, ROWS, ROWS), F32),
         ((2, 256, 256), F32),
         ((256, 256), F32),

time: 49.8 us -> 47.6 us (0.956)
  Pallas kernels: 49 us -> 46.7 us
    pallas_call x1, Pallas kernels: 47 us -> 44.8 us  [local(): pl.pallas_call(kernel, out_shape=out_shape, in_specs=[far] * 7, out_specs...]
where the time goes in v4:
time: 47.6 us; the launch traced here: 47.4 us
  Pallas kernels  46.7 us (98%)
  between operations  0.64 us (1%)
    pallas_call x1, Pallas kernels, local(): pl.pallas_call(kernel, out_shape=out_shape, in_specs=[far] * 7, out_specs...  44.8 us
    pallas_call x1, Pallas kernels, local(): pl.pallas_call(finish, out_shape=out_shape, in_specs=[far] * 5, out_specs...  1.99 us

profile of v4, /device:TPU:56, one launch (start us, length us, event | category | flops | bytes accessed | tf_op | source)
XLA Modules:
  0.0 47.4 jit_solution(13532779110716593941)
XLA Ops:
  0.6 44.8 %dilated_attention.1 = (bf16[128,768]{1,0:T(8,128)(2,1)}, bf16[128,768]{1,0:T(8,128)(2,1)}, bf16[128,768]{1,0:T(8,128)(2,1)}, bf16[128,768]{1,0:T(8,128)(2,1)}, f32[6,768]{1,0:T(8,128)}) custom-call(bf16[128,768]{1,0:T(8,128)(2,1)} %q_far.1, bf16[128,768]{1,0:T(8,128)(2,1)} %k_far.1, bf16[128,768]{1,0:T(8,128)(2,1)} %v_far.1, bf16[128,768]{1,0:T(8,128)(2,1)} %cot_far.1, ...), custom_call_target="tpu_custom_call" | custom-call | tf_op jit(solution)/shard_map/dilated_attention/pallas_call | solution.py:798
  45.4 2.0 %results_to_hbm.1 = (bf16[128,768]{1,0:T(8,128)(2,1)}, bf16[128,768]{1,0:T(8,128)(2,1)}, bf16[128,768]{1,0:T(8,128)(2,1)}, bf16[128,768]{1,0:T(8,128)(2,1)}, f32[6,768]{1,0:T(8,128)}) custom-call(bf16[128,768]{1,0:T(8,128)(2,1)} %get-tuple-element.10.refs_0_, bf16[128,768]{1,0:T(8,128)(2,1)} %get-tuple-element.11.refs_1_, ...), custom_call_target="tpu_custom_call" | custom-call | tf_op jit(solution)/shard_map/results_to_hbm/pallas_call | solution.py:814

commit v5 on v4

--- a/solution.py
+++ b/solution.py
@@ -15,6 +15,7 @@
 COUNT = (ROWS // 4, ROWS // 16)
 SCALE = DIM**-0.5
 HIDDEN = -1e30
+FIRST = 8
 EARLY = (0, 3, 5, 7)
 VMEM = 60 * 1024 * 1024
 F32 = jnp.float32
@@ -358,7 +359,7 @@
                 inside = (columns >= first) & (columns < first + DIM)
                 tiles[tile] = jnp.where(inside, piece, tiles[tile])
 
-    for head in range(HEADS):
+    def one_forward(head):
         lanes, first, span = window(head)
         scores = matmul(masked(q_ref[:, lanes], first, DIM), k_ref[:, lanes], (1, 1)) * SCALE
         scores = jnp.where(visible_one, scores, HIDDEN)
@@ -370,9 +371,9 @@
         merge(outs, head, out, True)
         merge(tops, head, top, False)
         merge(sums, head, total, False)
-    for tile in range(TILES):
-        level_out[0, tile] = outs[tile] / sums[tile]
-        level_lse[0, tile] = tops[tile] + jnp.log(sums[tile])
+
+    for head in range(FIRST):
+        one_forward(head)
 
     def split_three():
         both = recv_three[...].astype(F32).reshape(32, 2, 8, 128)
@@ -446,6 +447,12 @@
         push(d_send_two.at[other], d_recv_two.at[pl.ds(32 * mine_two, 32)], 12, block + other)
 
     keep(d_send_two.at[mine_two], d_recv_two.at[pl.ds(32 * mine_two, 32)], 12)
+
+    for head in range(FIRST, HEADS):
+        one_forward(head)
+    for tile in range(TILES):
+        level_out[0, tile] = outs[tile] / sums[tile]
+        level_lse[0, tile] = tops[tile] + jnp.log(sums[tile])
 
     arrived(out_recv_three, 3)
     out_three = put_windows([out_recv_three[head] for head in range(HEADS)], DIM, 0)

time: 47.6 us -> 47.5 us (level)
  no operation moved by 1% of the time
where the time goes in v5:
time: 47.5 us; the launch traced here: 47.4 us
  Pallas kernels  46.7 us (98%)
  between operations  0.64 us (1%)
    pallas_call x1, Pallas kernels, local(): pl.pallas_call(kernel, out_shape=out_shape, in_specs=[far] * 7, out_specs...  44.7 us
    pallas_call x1, Pallas kernels, local(): pl.pallas_call(finish, out_shape=out_shape, in_specs=[far] * 5, out_specs...  1.99 us

profile of v5, /device:TPU:56, one launch (start us, length us, event | category | flops | bytes accessed | tf_op | source)
XLA Modules:
  0.0 47.4 jit_solution(12509106956711912084)
XLA Ops:
  0.6 44.7 %dilated_attention.1 = (bf16[128,768]{1,0:T(8,128)(2,1)}, bf16[128,768]{1,0:T(8,128)(2,1)}, bf16[128,768]{1,0:T(8,128)(2,1)}, bf16[128,768]{1,0:T(8,128)(2,1)}, f32[6,768]{1,0:T(8,128)}) custom-call(bf16[128,768]{1,0:T(8,128)(2,1)} %q_far.1, bf16[128,768]{1,0:T(8,128)(2,1)} %k_far.1, bf16[128,768]{1,0:T(8,128)(2,1)} %v_far.1, bf16[128,768]{1,0:T(8,128)(2,1)} %cot_far.1, ...), custom_call_target="tpu_custom_call" | custom-call | tf_op jit(solution)/shard_map/dilated_attention/pallas_call | solution.py:805
  45.4 2.0 %results_to_hbm.1 = (bf16[128,768]{1,0:T(8,128)(2,1)}, bf16[128,768]{1,0:T(8,128)(2,1)}, bf16[128,768]{1,0:T(8,128)(2,1)}, bf16[128,768]{1,0:T(8,128)(2,1)}, f32[6,768]{1,0:T(8,128)}) custom-call(bf16[128,768]{1,0:T(8,128)(2,1)} %get-tuple-element.10.refs_0_, bf16[128,768]{1,0:T(8,128)(2,1)} %get-tuple-element.11.refs_1_, ...), custom_call_target="tpu_custom_call" | custom-call | tf_op jit(solution)/shard_map/results_to_hbm/pallas_call | solution.py:821
